TPU v7x, 32 devices: a whole 2x2x4 slice. The times are simulated.
32 devices in a mesh: frame: 8 (over z, x), strip: 4 (over y, core).
Axes of the slice: x: 2, y: 2, z: 4, core: 2. Of those that a mesh axis runs over, the one named last changes fastest.
Arguments:
- movie: bfloat16 [64, 256, 2048], P('frame', 'strip'), may hold values from -17 to 22, as said below
Outputs:
- lag_maps: float32 [25, 256, 2048], P(None, 'strip', 'frame')
Inputs may be any that keep to these rules, and one draw needn't show every extreme that they name: Frames of a camera movie.
All inputs are finite; a program needn't handle non-finite values.
Results may differ from a plain program's by a relative error of at most 0.0004.
Values may be sent and summed in bfloat16 or wider, within the bound.
No kernel may reach another device: no remote copies, remote signals or barrier semaphores. Data moves between devices by JAX's collectives and lax.ppermute only.
A program may use at most 64 MiB of HBM per device.

v0:
```python
import jax
import jax.numpy as jnp
from jax import lax
from jax.sharding import PartitionSpec as P


def padded(value, sides, width):
    for axis, dim in sides:
        peers, length = (lax.axis_size(axis), value.shape[dim])
        up = [(i, (i + 1) % peers) for i in range(peers - 1)]
        down = [(j, i) for i, j in up]
        last = lax.slice_in_dim(value, length - width, length, axis=dim)
        initial = lax.slice_in_dim(value, 0, width, axis=dim)
        before = lax.ppermute(last, axis, up)
        after = lax.ppermute(initial, axis, down)
        value = jnp.concatenate([before, value, after], axis=dim)
    return value


def lag_products(field, rows, columns):
    centre = field[:, 2 : 2 + rows, 2 : 2 + columns]
    products = []
    for row_lag in range(-2, 3):
        for col_lag in range(-2, 3):
            shifted = field[
                :, 2 + row_lag : 2 + row_lag + rows, 2 + col_lag : 2 + col_lag + columns
            ]
            products.append(jnp.sum(centre * shifted, axis=0))
    return jnp.stack(products)


def body(movie):
    frames_here, rows, width = movie.shape
    frame_count = lax.axis_size("frame")
    frames_total = frames_here * frame_count
    columns = width // frame_count
    moved = lax.all_to_all(movie, "frame", split_axis=2, concat_axis=0, tiled=True)
    widened = padded(moved, (("strip", 1), ("frame", 2)), 2)
    raw_values = widened.astype(jnp.float32)
    pixel_mean = jnp.sum(raw_values, axis=0) / frames_total
    return lag_products(raw_values - pixel_mean, rows, columns) / frames_total


def solution(mesh):
    return jax.shard_map(
        body,
        mesh=mesh,
        in_specs=(P("frame", "strip", None),),
        out_specs=P(None, "strip", "frame"),
        check_vma=False,
    )
```

profile of v0, /device:TPU:11, one launch (start us, length us, event | category | flops | bytes accessed | tf_op | source)
XLA Modules:
  0.0 167.5 jit_solution(4740184157223663381)
XLA Ops:
  0.0 5.6 %copy.3 = bf16[8,64,2048]{1,0,2:T(8,128)(2,1)} copy(bf16[8,64,2048]{2,1,0:T(8,128)(2,1)} %param.1) | data formatting | bytes 4194304 | tf_op args[0]
  5.6 6.4 %reshape.3 = bf16[8,2,65536]{2,1,0:T(2,128)(2,1)S(1)} reshape(bf16[2048,8,64]{2,1,0:T(8,128)(2,1)} %bitcast.62) | data formatting | bytes 4194304
  12.0 50.7 %all_to_all.18 = bf16[8,2,65536]{2,1,0:T(2,128)(2,1)} all-to-all(bf16[8,2,65536]{2,1,0:T(2,128)(2,1)S(1)} %reshape.3), channel_id=1, replica_groups=mesh['frame'=8,'strip'=4] {'frame'}, dimensions={0} | all-to-all | bytes 4194304 | tf_op jit(solution)/shard_map/all_to_all | solution.py:37
  62.7 7.4 %reshape.4 = bf16[2048,8,64]{2,1,0:T(8,128)(2,1)} reshape(bf16[8,2,65536]{2,1,0:T(2,128)(2,1)} %all_to_all.18) | data formatting | bytes 4194304
  70.1 4.0 %copy.5 = bf16[8,8,64,256]{3,2,1,0:T(8,128)(2,1)S(1)} copy(bf16[8,8,64,256]{2,1,3,0:T(8,128)(2,1)} %bitcast.61) | data formatting | bytes 4194304 | tf_op jit(solution)/shard_map/all_to_all | solution.py:37
  74.1 0.1 fusion.25
  74.2 5.2 %collective-permute-start = (bf16[64,2,256]{2,1,0:T(2,128)(2,1)S(1)}, bf16[64,2,256]{2,1,0:T(2,128)(2,1)S(1)}, u32[]{:S(2)}, u32[]{:S(2)}) collective-permute-start(bf16[64,2,256]{2,1,0:T(2,128)(2,1)S(1)} %get-tuple-element.38), channel_id=1, source_target_pairs={{0,1},{1,2},{2,3},{4,5},{5,6},{6,7},{8,9},{9,10},{10,11},{12,13},{... | collective-permute-start | bytes 196616 | tf_op jit(solution)/shard_map/ppermute | solution.py:14
  79.5 1.9 %collective-permute-start.1 = (bf16[64,2,256]{2,1,0:T(2,128)(2,1)S(1)}, bf16[64,2,256]{2,1,0:T(2,128)(2,1)S(1)}, u32[]{:S(2)}, u32[]{:S(2)}) collective-permute-start(bf16[64,2,256]{2,1,0:T(2,128)(2,1)S(1)} %get-tuple-element.39), channel_id=1, source_target_pairs={{1,0},{2,1},{3,2},{5,4},{6,5},{7,6},{9,8},{10,9},{11,10},{13,12},{... | collective-permute-start | bytes 196616 | tf_op jit(solution)/shard_map/ppermute | solution.py:15
  81.4 0.0 collective-permute-done
  81.4 3.6 %collective-permute-done.1 = bf16[64,2,256]{2,1,0:T(2,128)(2,1)S(1)} collective-permute-done((bf16[64,2,256]{2,1,0:T(2,128)(2,1)S(1)}, bf16[64,2,256]{2,1,0:T(2,128)(2,1)S(1)}, u32[]{:S(2)}, u32[]{:S(2)}) %collective-permute-start.1) | collective-permute-done | bytes 65568 | tf_op jit(solution)/shard_map/ppermute | solution.py:15
  85.0 1.5 pad_maximum_fusion.1
  86.5 1.6 fusion.24
  88.1 1.8 %copy.6 = bf16[64,68,2]{1,0,2:T(8,128)(2,1)S(1)} copy(bf16[64,68,2]{2,1,0:T(8,128)(2,1)} %get-tuple-element.36) | data formatting | bytes 34816 | tf_op jit(solution)/shard_map/slice | solution.py:12
  89.9 3.4 %collective-permute-start.2 = (bf16[64,68,2]{1,0,2:T(8,128)(2,1)S(1)}, bf16[64,68,2]{1,0,2:T(8,128)(2,1)S(1)}, u32[]{:S(2)}, u32[]{:S(2)}) collective-permute-start(bf16[64,68,2]{1,0,2:T(8,128)(2,1)S(1)} %copy.6), channel_id=1, source_target_pairs={{0,4},{4,8},{8,12},{12,16},{16,20},{20,24},{24,28},{1,5},{5,9},{9,... | collective-permute-start | bytes 52232 | tf_op jit(solution)/shard_map/ppermute | solution.py:14
  93.3 0.6 copy.7
  93.8 2.1 %collective-permute-start.3 = (bf16[64,68,2]{1,0,2:T(8,128)(2,1)S(1)}, bf16[64,68,2]{1,0,2:T(8,128)(2,1)S(1)}, u32[]{:S(2)}, u32[]{:S(2)}) collective-permute-start(bf16[64,68,2]{1,0,2:T(8,128)(2,1)S(1)} %copy.7), channel_id=1, source_target_pairs={{4,0},{8,4},{12,8},{16,12},{20,16},{24,20},{28,24},{5,1},{9,5},{13... | collective-permute-start | bytes 52232 | tf_op jit(solution)/shard_map/ppermute | solution.py:15
  96.0 0.0 collective-permute-done.2
  96.0 0.6 copy.8
  96.6 2.8 %collective-permute-done.3 = bf16[64,68,2]{1,0,2:T(8,128)(2,1)S(1)} collective-permute-done((bf16[64,68,2]{1,0,2:T(8,128)(2,1)S(1)}, bf16[64,68,2]{1,0,2:T(8,128)(2,1)S(1)}, u32[]{:S(2)}, u32[]{:S(2)}) %collective-permute-start.3) | collective-permute-done | bytes 17440 | tf_op jit(solution)/shard_map/ppermute | solution.py:15
  99.4 1.6 copy.9
  101.0 0.0 copy-start.1
  101.0 5.2 %convert_reduce_fusion = f32[68,260]{1,0:T(8,128)S(1)} fusion(bf16[64,68,2]{2,1,0:T(8,128)(2,1)} %copy.9, bf16[64,2,256]{2,1,0:T(2,128)(2,1)S(1)} %collective-permute-done.1, bf16[64,64,256]{2,1,0:T(8,128)(2,1)S(1)} %bitcast.59, bf16[64,2,256]{2,1,0:T(2,128)(2,1)S(1)} %collective-permute-done, bf16[64,68,2]{2,1,0:T(8,128)(2,1)S(1)} %copy.8), kind=kLoop, calls=%fused_computation.1 | loop fusion | flops 12429040 | bytes 2333760 | tf_op jit(solution)/shard_map/reduce_sum | solution.py:40
  106.2 0.0 copy-done.1
  106.2 3.7 %convert_subtract_fusion = f32[64,68,260]{2,1,0:T(8,128)S(1)} fusion(f32[68,260]{1,0:T(8,128)S(1)} %broadcast_multiply_fusion.1, bf16[64,68,2]{2,1,0:T(8,128)(2,1)S(1)} %copy-done.1, bf16[64,2,256]{2,1,0:T(2,128)(2,1)S(1)} %collective-permute-done.1, bf16[64,64,256]{2,1,0:T(8,128)(2,1)S(1)} %bitcast.60, bf16[64,2,256]{2,1,0:T(2,128)(2,1)S(1)} %collective-permute-done, ...), kind=kLoop, calls=%fused_computation | loop fusion | flops 12446720 | bytes 6859840 | tf_op jit(solution)/shard_map/sub | solution.py:41
  109.9 0.0 copy-start
  109.9 2.9 %copy-done = f32[64,68,260]{2,1,0:T(8,128)} copy-done((f32[64,68,260]{2,1,0:T(8,128)}, f32[64,68,260]{2,1,0:T(8,128)S(1)}, u32[]{:S(2)}) %copy-start) | copy-done | bytes 4526104
  112.8 9.1 %fusion.9 = (f32[64,256]{1,0:T(8,128)S(1)}, f32[64,256]{1,0:T(8,128)S(1)}, f32[64,256]{1,0:T(8,128)S(1)}, f32[64,256]{1,0:T(8,128)S(1)}, f32[64,256]{1,0:T(8,128...) fusion(f32[64,68,260]{2,1,0:T(8,128)S(1)} %convert_subtract_fusion), kind=kLoop, calls=%fused_computation.21 | loop fusion | flops 18726912 | bytes 42532864 | tf_op jit(solution)/shard_map/reduce_sum | solution.py:28
  121.9 43.9 %fusion = (f32[64,256]{1,0:T(8,128)S(1)}, f32[64,256]{1,0:T(8,128)S(1)}, f32[64,256]{1,0:T(8,128)S(1)}, f32[64,256]{1,0:T(8,128)S(1)}, f32[64,256]{1,0:T(8,128)S...) fusion(f32[64,68,260]{2,1,0:T(8,128)} %copy-done), kind=kLoop, calls=%fused_computation.3 | loop fusion | flops 33292288 | bytes 68157440 | tf_op jit(solution)/shard_map/reduce_sum | solution.py:28
  166.2 1.3 broadcast_multiply_fusion
  (26 shorter events, 0.2 us)
Async XLA Ops:
  74.2 7.2 %collective-permute-start = (bf16[64,2,256]{2,1,0:T(2,128)(2,1)S(1)}, bf16[64,2,256]{2,1,0:T(2,128)(2,1)S(1)}, u32[]{:S(2)}, u32[]{:S(2)}) collective-permute-start(bf16[64,2,256]{2,1,0:T(2,128)(2,1)S(1)} %get-tuple-element.38), channel_id=1, source_target_pairs={{0,1},{1,2},{2,3},{4,5},{5,6},{6,7},{8,9},{9,10},{10,11},{12,13},{... | collective-permute-start | bytes 196616 | tf_op jit(solution)/shard_map/ppermute | solution.py:14
  79.5 5.6 %collective-permute-start.1 = (bf16[64,2,256]{2,1,0:T(2,128)(2,1)S(1)}, bf16[64,2,256]{2,1,0:T(2,128)(2,1)S(1)}, u32[]{:S(2)}, u32[]{:S(2)}) collective-permute-start(bf16[64,2,256]{2,1,0:T(2,128)(2,1)S(1)} %get-tuple-element.39), channel_id=1, source_target_pairs={{1,0},{2,1},{3,2},{5,4},{6,5},{7,6},{9,8},{10,9},{11,10},{13,12},{... | collective-permute-start | bytes 196616 | tf_op jit(solution)/shard_map/ppermute | solution.py:15
  89.9 6.1 %collective-permute-start.2 = (bf16[64,68,2]{1,0,2:T(8,128)(2,1)S(1)}, bf16[64,68,2]{1,0,2:T(8,128)(2,1)S(1)}, u32[]{:S(2)}, u32[]{:S(2)}) collective-permute-start(bf16[64,68,2]{1,0,2:T(8,128)(2,1)S(1)} %copy.6), channel_id=1, source_target_pairs={{0,4},{4,8},{8,12},{12,16},{16,20},{20,24},{24,28},{1,5},{5,9},{9,... | collective-permute-start | bytes 52232 | tf_op jit(solution)/shard_map/ppermute | solution.py:14
  93.8 5.6 %collective-permute-start.3 = (bf16[64,68,2]{1,0,2:T(8,128)(2,1)S(1)}, bf16[64,68,2]{1,0,2:T(8,128)(2,1)S(1)}, u32[]{:S(2)}, u32[]{:S(2)}) collective-permute-start(bf16[64,68,2]{1,0,2:T(8,128)(2,1)S(1)} %copy.7), channel_id=1, source_target_pairs={{4,0},{8,4},{12,8},{16,12},{20,16},{24,20},{28,24},{5,1},{9,5},{13... | collective-permute-start | bytes 52232 | tf_op jit(solution)/shard_map/ppermute | solution.py:15
  101.0 5.2 %copy-start.1 = (bf16[64,68,2]{2,1,0:T(8,128)(2,1)S(1)}, bf16[64,68,2]{2,1,0:T(8,128)(2,1)}, u32[]{:S(2)}) copy-start(bf16[64,68,2]{2,1,0:T(8,128)(2,1)} %copy.9) | copy-start | bytes 52228
  109.9 2.9 %copy-start = (f32[64,68,260]{2,1,0:T(8,128)}, f32[64,68,260]{2,1,0:T(8,128)S(1)}, u32[]{:S(2)}) copy-start(f32[64,68,260]{2,1,0:T(8,128)S(1)} %convert_subtract_fusion) | copy-start | bytes 13578244
where the time goes:
time: 169 us; the launch traced here: 167 us
  other arithmetic  64.6 us (38%)
  blocking collectives  50.7 us (30%)
  local copies, waits for them, and re-layouts  32.7 us (19%)
  starting transfers between devices  12.7 us (8%)
  waiting for transfers between devices  6.45 us (4%)
    reduce_sum x2, other arithmetic, lag_products(): products.append(jnp.sum(centre * shifted, axis=0))  53 us
    all_to_all x1, blocking collectives, body(): lax.all_to_all(movie, 'frame', split_axis=2, concat_axis=0, tiled=True)  50.7 us
    unnamed x31, local copies, waits for them, and re-layouts  22.5 us
    ppermute x2, starting transfers between devices, padded(): before = lax.ppermute(last, axis, up)  8.64 us
    ppermute x2, waiting for transfers between devices, padded(): after = lax.ppermute(initial, axis, down)  6.44 us
    reduce_sum x1, other arithmetic, body(): pixel_mean = jnp.sum(raw_values, axis=0) / frames_total  5.16 us
    ppermute x2, starting transfers between devices, padded(): after = lax.ppermute(initial, axis, down)  4.06 us
    all_to_all x1, local copies, waits for them, and re-layouts, body(): lax.all_to_all(movie, 'frame', split_axis=2, concat_axis=0, tiled=True)  4.01 us
  transfers between devices with their start and end apart: 4, of which 2 were waited for; matrix products, arithmetic and copies ran while one was open for 1% of the time, Pallas kernels for 0%

commit v1 on v0

v1 whole, which is shorter than its diff:
```python
import jax
import jax.numpy as jnp
from jax import lax
from jax.experimental import pallas as pl
from jax.experimental.pallas import tpu as pltpu
from jax.sharding import PartitionSpec as P

REACH = 2
LANES = 128
GROUP = 8
PAIR = 2 * GROUP
LAG_LIST = tuple(
    (a, b)
    for a in range(REACH + 1)
    for b in range(-REACH, REACH + 1)
    if a > 0 or b >= 0
)
VMEM = 56 * 1024 * 1024


def shifted(ring, index, offset):
    tile = ring[index]
    if offset == 0:
        return tile
    lane = lax.broadcasted_iota(jnp.int32, tile.shape, tile.ndim - 1)
    if offset > 0:
        other = ring[(index + 1) % len(ring)]
        mixed = jnp.where(lane < offset, other, tile)
    else:
        other = ring[index - 1]
        mixed = jnp.where(lane >= LANES + offset, other, tile)
    return pltpu.roll(mixed, (-offset) % LANES, 1)


def both_rows(ref, index, row, stride):
    return jnp.concatenate(
        [ref[index, pl.ds(row + j, GROUP, stride=stride), :] for j in range(2)], axis=0
    )


def write_packed(ref, places, rows, outs):
    lane = lax.broadcasted_iota(jnp.int32, (PAIR, LANES), 1)
    zero = jnp.zeros((PAIR, LANES), jnp.float32)

    def pair(q, edges):
        result = []
        for (own, left, right), out, edge in zip(places, outs, edges):
            for t, place in enumerate(own):
                start = pl.multiple_of((t * rows + 2 * q) * GROUP, PAIR)
                both = both_rows(ref, place, 2 * q, rows)
                out[pl.ds(start, PAIR), :] = both.astype(jnp.bfloat16)
            sides = jnp.where(
                lane >= LANES - REACH,
                both_rows(ref, left, 2 * q, rows),
                both_rows(ref, right, 2 * q, rows),
            )
            first = 2 * REACH * q
            placed = pltpu.roll(sides, first + REACH, 1)
            inside = (lane >= first) & (lane < first + 2 * REACH)
            result.append(jnp.where(inside, placed, edge))
        return tuple(result)

    edges = lax.fori_loop(0, rows // 2, pair, (zero,) * len(outs), unroll=4)
    for (own, _, _), out, edge in zip(places, outs, edges):
        out[len(own) * rows * GROUP :, :] = edge.astype(jnp.bfloat16)


def pack_one_kernel(tiles, block_ref, main_ref, left_ref, right_ref, out_ref, values):
    frames, rows, _ = main_ref.shape
    block, blocks = block_ref[0], block_ref[1]
    flat = (frames * rows, LANES)
    for t in range(tiles):
        part = main_ref[:, :, t * LANES : (t + 1) * LANES]
        values[t] = part.astype(jnp.float32).reshape(flat)
    left = left_ref[...].astype(jnp.float32).reshape(flat)
    right = right_ref[...].astype(jnp.float32).reshape(flat)
    values[tiles] = jnp.where(block > 0, left, 0.0)
    values[tiles + 1] = jnp.where(block < blocks - 1, right, 0.0)
    places = [(list(range(tiles)), tiles, tiles + 1)]
    write_packed(values, places, rows, [out_ref])


def packed_length(rows, tiles):
    return tiles * rows * GROUP + PAIR


def pack_one(movie, block, blocks):
    frames, rows, width = movie.shape
    columns = width // blocks
    tiles = columns // LANES
    last = width // LANES - 1
    length = packed_length(rows, tiles)
    return pl.pallas_call(
        lambda *refs: pack_one_kernel(tiles, *refs),
        out_shape=jax.ShapeDtypeStruct((length, LANES), jnp.bfloat16),
        grid_spec=pltpu.PrefetchScalarGridSpec(
            num_scalar_prefetch=1,
            grid=(1,),
            in_specs=[
                pl.BlockSpec((frames, rows, columns), lambda i, s: (0, 0, s[0])),
                pl.BlockSpec(
                    (frames, rows, LANES),
                    lambda i, s: (0, 0, jnp.maximum(s[0] * tiles - 1, 0)),
                ),
                pl.BlockSpec(
                    (frames, rows, LANES),
                    lambda i, s: (0, 0, jnp.minimum(s[0] * tiles + tiles, last)),
                ),
            ],
            out_specs=pl.BlockSpec((length, LANES), lambda i, s: (0, 0)),
            scratch_shapes=[pltpu.VMEM((tiles + 2, frames * rows, LANES), jnp.float32)],
        ),
        compiler_params=pltpu.CompilerParams(vmem_limit_bytes=VMEM),
        name="pack_one",
    )(jnp.stack([block, jnp.int32(blocks)]), movie, movie, movie)


def pack_kernel(tiles, me_ref, movie_ref, *refs):
    outs, values = refs[:-1], refs[-1]
    frames, rows, width = movie_ref.shape
    count = width // LANES
    blocks = count // tiles
    flat = (frames * rows, LANES)
    zero = jnp.zeros(flat, jnp.float32)
    values[0] = zero
    values[count + 1] = zero
    for t in range(count):
        part = movie_ref[:, :, t * LANES : (t + 1) * LANES]
        values[t + 1] = part.astype(jnp.float32).reshape(flat)
    places = []
    for k in range(blocks):
        if outs[k] is None:
            continue
        first = 1 + (me_ref[0] ^ k) * tiles
        places.append(([first + t for t in range(tiles)], first - 1, first + tiles))
    write_packed(values, places, rows, [out for out in outs if out is not None])


def pack_rest(movie, me, blocks, skip):
    frames, rows, width = movie.shape
    tiles = width // blocks // LANES
    length = packed_length(rows, tiles)
    whole = pl.BlockSpec(memory_space=pltpu.VMEM)
    kept = [k for k in range(blocks) if k != skip]

    def kernel(me_ref, movie_ref, *refs):
        outs = list(refs[:-1])
        outs.insert(skip, None)
        pack_kernel(tiles, me_ref, movie_ref, *outs, refs[-1])

    results = pl.pallas_call(
        kernel,
        out_shape=[jax.ShapeDtypeStruct((length, LANES), jnp.bfloat16)] * len(kept),
        in_specs=[pl.BlockSpec(memory_space=pltpu.SMEM), whole],
        out_specs=[whole] * len(kept),
        scratch_shapes=[
            pltpu.VMEM((width // LANES + 2, frames * rows, LANES), jnp.float32)
        ],
        compiler_params=pltpu.CompilerParams(vmem_limit_bytes=VMEM),
        name="pack_rest",
    )(me[None], movie)
    return dict(zip(kept, results))


def lag_kernel(tiles, rows, frames, sources, has_prior, last, *refs):
    refs = list(refs)
    blocks = [refs[3 * i : 3 * i + 3] for i in range(sources + 1)]
    refs = refs[3 * sources + 3 :]
    prior = None
    if has_prior:
        prior, prior_sum = refs[:2]
        refs = refs[2:]
    if last:
        out, rings, shifts, parts, maps, sums, sum_shifts, cov = refs
    else:
        maps, sums, rings, shifts, parts = refs
    ring = tiles + 1
    span = (rows + 2 * REACH) * GROUP

    def unfold(edge, index):
        return pltpu.roll(edge, (-2 * REACH * index - REACH) % LANES, 1)

    def place(i, t, start, value):
        if i == 0:
            value = jnp.concatenate(
                [
                    jnp.broadcast_to(value[j * GROUP : j * GROUP + 1], (GROUP, LANES))
                    for j in range(2)
                ],
                axis=0,
            )
        rings[i, t, pl.ds(start, PAIR), :] = value.astype(jnp.bfloat16)

    main = tiles * rows * GROUP
    for i, (body, above, below) in enumerate(blocks):
        for ref, start, index in ((above, 0, rows // 2 - 1), (below, span - PAIR, 0)):
            for t in range(tiles):
                value = ref[t * PAIR : (t + 1) * PAIR, :].astype(jnp.float32)
                place(i, t, start, value)
            edge = ref[tiles * PAIR :, :].astype(jnp.float32)
            place(i, tiles, start, unfold(edge, index))
        if i > 0:
            for t in range(tiles):
                part = body[t * rows * GROUP : (t + 1) * rows * GROUP, :]
                rings[i, t, PAIR : span - PAIR, :] = part

    tails = [b[0][main:, :].astype(jnp.float32) for b in blocks]

    def fill(q, carry):
        start = pl.multiple_of((q + 1) * PAIR, PAIR)
        shift = lax.rem(2 * LANES - 2 * REACH * q - REACH, LANES)
        for i, (body, _, _) in enumerate(blocks):
            place(i, tiles, start, pltpu.roll(tails[i], shift, 1))
            if i == 0:
                for t in range(tiles):
                    at = pl.multiple_of(t * rows * GROUP + q * PAIR, PAIR)
                    place(i, t, start, body[pl.ds(at, PAIR), :].astype(jnp.float32))
        return carry

    lax.fori_loop(0, rows // 2, fill, 0, unroll=4)

    source = lax.broadcasted_iota(jnp.int32, (2 * LANES, LANES), 0)
    target = lax.broadcasted_iota(jnp.int32, (2 * LANES, LANES), 1)
    moves = jnp.concatenate(
        [jnp.where(source == target + b, 1.0, 0.0) for b in range(1, REACH + 1)], axis=1
    ).astype(jnp.bfloat16)
    size = (rows + 2 * REACH) * GROUP // (2 if sources < 3 else 17)
    if size % PAIR or span % size:
        size = PAIR

    def spread(c, carry):
        at = pl.ds(pl.multiple_of(c * size, PAIR), size)
        raw = [[rings[i, t, at, :] for t in range(ring)] for i in range(sources + 1)]
        wide = jnp.concatenate(
            [
                jnp.concatenate([r[t], r[(t + 1) % ring]], axis=1)
                for r in raw
                for t in range(ring)
            ],
            axis=0,
        )
        moved = jnp.dot(wide, moves, preferred_element_type=jnp.float32)

        def version(i, t, b):
            if b == 0:
                return raw[i][t].astype(jnp.float32)
            first = (i * ring + t) * size
            return moved[first : first + size, (b - 1) * LANES : b * LANES]

        for t in range(ring):
            for b in range(REACH + 1):
                pivot = version(0, t, b)
                for i in range(1, sources + 1):
                    shifts[b, i - 1, t, at, :] = version(i, t, b) - pivot
        return carry

    lax.fori_loop(0, span // size, spread, 0)

    def products(t, slot, lags):
        totals = [[None] * (len(lags) + 1) for _ in range(2)]
        for i in range(sources):
            cache = {}

            def value(step, offset):
                if (step, offset) not in cache:
                    start = pl.multiple_of((slot + step) * GROUP, GROUP)
                    cache[step, offset] = shifts[offset, i, t, pl.ds(start, GROUP), :]
                return cache[step, offset]

            for j in range(2):
                for k, (a, b) in enumerate(lags):
                    term = value(j, max(-b, 0)) * value(j + a, max(b, 0))
                    totals[j][k] = term if i == 0 else totals[j][k] + term
                term = value(j, 0)
                totals[j][-1] = term if i == 0 else totals[j][-1] + term
        return totals

    def folded(k, first):
        terms = [
            parts[k, pl.ds(first + u, GROUP, stride=GROUP), :] for u in range(GROUP)
        ]
        while len(terms) > 1:
            terms = [x + y for x, y in zip(terms[::2], terms[1::2])]
        return terms[0]

    count = len(LAG_LIST)
    lead = GROUP - REACH
    for k in range(count + 1):
        parts[k, : lead * GROUP, :] = jnp.zeros((lead * GROUP, LANES), jnp.float32)
    for t in range(ring):
        wanted = [k for k, (a, b) in enumerate(LAG_LIST) if t < tiles or b != 0]
        lags = [LAG_LIST[k] for k in wanted]

        def pair(q, carry):
            totals = products(t, 2 * q, lags)
            for j in range(2):
                at = pl.ds(pl.multiple_of((lead + 2 * q + j) * GROUP, GROUP), GROUP)
                for n, k in enumerate(wanted + [count]):
                    parts[k, at, :] = totals[j][n]
            return carry

        lax.fori_loop(0, rows // 2 + 1, pair, 0)

        def reduce(g, carry):
            at = pl.ds(pl.multiple_of(g * GROUP, GROUP), GROUP)
            for k in wanted:
                value = folded(k, g * GROUP * GROUP)
                if has_prior:
                    value = value + prior[k, t, at, :]
                maps[k, t, at, :] = value
            value = folded(count, g * GROUP * GROUP)
            if has_prior:
                value = value + prior_sum[t, at, :]
            sums[t, at, :] = value
            return carry

        lax.fori_loop(0, rows // GROUP + 1, reduce, 0)
        for j in range(GROUP):
            start = (rows + min(REACH + j, 2 * REACH - 1)) * GROUP
            v = shifts[0, 0, t, start : start + GROUP, :]
            for i in range(1, sources):
                v = v + shifts[0, i, t, start : start + GROUP, :]
            parts[count, (rows + GROUP + j) * GROUP : (rows + GROUP + j + 1) * GROUP] = v
        value = folded(count, (rows + GROUP) * GROUP)
        if has_prior:
            value = value + prior_sum[t, rows + GROUP :, :]
        sums[t, rows + GROUP :, :] = value

    if last:
        finish(tiles, rows, frames, maps, sums, out, sum_shifts, cov)


def finish(tiles, rows, frames, maps, sums, out, sum_shifts, cov):
    ring = tiles + 1
    scale = 1.0 / frames
    for g in range((rows + 2 * GROUP) // GROUP):
        at = slice(g * GROUP, (g + 1) * GROUP)
        row_ring = [sums[t, at, :] for t in range(ring)]
        for t in range(ring):
            for b in range(REACH + 1):
                sum_shifts[b, t, at, :] = shifted(row_ring, t, b)

    def centred(g, carry):
        start = pl.multiple_of(g * GROUP, GROUP)
        at = pl.ds(start, GROUP)
        for t in range(ring):
            here = [sum_shifts[b, t, at, :] * scale for b in range(REACH + 1)]
            for k, (a, b) in enumerate(LAG_LIST):
                if t == tiles and b == 0:
                    continue
                other = sum_shifts[max(b, 0), t, pl.ds(start + a, GROUP), :]
                mean = here[max(-b, 0)]
                cov[k, t, at, :] = (maps[k, t, at, :] - mean * other) * scale
        return carry

    lax.fori_loop(0, rows // GROUP + 1, centred, 0)

    def write(g, carry):
        start = pl.multiple_of(g * GROUP, GROUP)
        here = pl.ds(start, GROUP)
        for k, (a, b) in enumerate(LAG_LIST):
            index = (2 * REACH + 1) * (a + REACH) + b + REACH
            mirror = (2 * REACH + 1) ** 2 - 1 - index
            for n, first, offset in (
                (index, start + GROUP, min(b, 0)),
                (mirror, start + GROUP - a, min(-b, 0)),
            ):
                row_ring = [
                    cov[k, t, pl.ds(first, GROUP), :] if t < tiles or offset else None
                    for t in range(ring)
                ]
                for t in range(tiles):
                    lanes = slice(t * LANES, (t + 1) * LANES)
                    out[n, here, lanes] = shifted(row_ring, t, offset)
                if index == mirror:
                    break
        return carry

    lax.fori_loop(0, rows // GROUP, write, 0)


def lag_sums(blocks, rows, tiles, frames, prior=None, last=False):
    sources = len(blocks) - 1
    ring = tiles + 1
    span = (rows + 2 * REACH) * GROUP
    operands = [a for block in blocks for a in block] + list(prior or ())
    whole = pl.BlockSpec(memory_space=pltpu.VMEM)
    map_shape = (len(LAG_LIST), ring, rows + GROUP, LANES)
    sum_shape = (ring, rows + 2 * GROUP, LANES)
    scratch = [
        pltpu.VMEM((sources + 1, ring, span, LANES), jnp.bfloat16),
        pltpu.VMEM((REACH + 1, sources, ring, span, LANES), jnp.float32),
        pltpu.VMEM((len(LAG_LIST) + 1, (rows + 2 * GROUP) * GROUP, LANES), jnp.float32),
    ]
    if last:
        out_shape = jax.ShapeDtypeStruct(
            ((2 * REACH + 1) ** 2, rows, tiles * LANES), jnp.float32
        )
        out_specs = whole
        scratch += [
            pltpu.VMEM(map_shape, jnp.float32),
            pltpu.VMEM(sum_shape, jnp.float32),
            pltpu.VMEM((REACH + 1,) + sum_shape, jnp.float32),
            pltpu.VMEM(map_shape, jnp.float32),
        ]
    else:
        out_shape = (
            jax.ShapeDtypeStruct(map_shape, jnp.float32),
            jax.ShapeDtypeStruct(sum_shape, jnp.float32),
        )
        out_specs = (whole, whole)
    return pl.pallas_call(
        lambda *refs: lag_kernel(
            tiles, rows, frames, sources, prior is not None, last, *refs
        ),
        out_shape=out_shape,
        in_specs=[whole] * len(operands),
        out_specs=out_specs,
        scratch_shapes=scratch,
        compiler_params=pltpu.CompilerParams(vmem_limit_bytes=VMEM),
        name="lag_maps" if last else "lag_sums",
    )(*operands)


def edge_blocks(packed, rows, tiles):
    size = rows * GROUP
    tail = packed[tiles * size :]
    first = [packed[t * size : t * size + PAIR] for t in range(tiles)]
    last = [packed[(t + 1) * size - PAIR : (t + 1) * size] for t in range(tiles)]
    return jnp.concatenate(first + [tail]), jnp.concatenate(last + [tail])


def exchange_rows(blocks, rows, tiles):
    strips = lax.axis_size("strip")
    up = [(i, i + 1) for i in range(strips - 1)]
    down = [(j, i) for i, j in up]
    pairs = [edge_blocks(b, rows, tiles) for b in blocks]
    above = lax.ppermute(jnp.stack([last for _, last in pairs]), "strip", up)
    below = lax.ppermute(jnp.stack([first for first, _ in pairs]), "strip", down)
    return [(above[i], below[i]) for i in range(len(blocks))]


def body(movie):
    frames_here, rows, width = movie.shape
    peers = lax.axis_size("frame")
    tiles = width // peers // LANES
    me = lax.axis_index("frame")
    frames = frames_here * peers
    half = peers // 2
    far = list(range(half, peers))
    near = list(range(1, half))
    packed = pack_rest(movie, me, peers, far[0])
    packed[far[0]] = pack_one(movie, me ^ far[0], peers)
    steps = far[:1] + near + far[1:]
    moved = {0: packed[0]}
    for k in steps:
        moved[k] = lax.ppermute(packed[k], "frame", [(i, i ^ k) for i in range(peers)])
    every = [0] + steps
    halos = exchange_rows([moved[k] for k in every], rows, tiles)
    blocks = [(moved[k],) + halo for k, halo in zip(every, halos)]
    half = len(blocks) // 2
    prior = lag_sums(blocks[:1] + blocks[:half], rows, tiles, frames)
    return lag_sums(blocks[:1] + blocks[half:], rows, tiles, frames, prior, True)


def solution(mesh):
    return jax.shard_map(
        body,
        mesh=mesh,
        in_specs=(P("frame", "strip", None),),
        out_specs=P(None, "strip", "frame"),
        check_vma=False,
    )
```

time: 169 us -> 89 us (0.53)
  other arithmetic: 64.6 us -> 0.81 us
  blocking collectives: 50.7 us -> 0 us
  Pallas kernels: 0 us -> 36.6 us
  local copies, waits for them, and re-layouts: 32.7 us -> 2.76 us
  waiting for transfers between devices: 6.45 us -> 33.9 us
    reduce_sum x3 -> x0, other arithmetic: 58.1 us -> none  [the longest x2 53 us: lag_products(): products.append(jnp.sum(centre * shifted, axis=0))]
    all_to_all x1 -> x0, blocking collectives: 50.7 us -> none  [body(): lax.all_to_all(movie, 'frame', split_axis=2, concat_axis=0, tiled=True)]
    pallas_call x0 -> x4, Pallas kernels: none -> 36.6 us  [the longest x2 25.2 us: lag_sums(): pl.pallas_call(lambda *refs: lag_kernel(tiles, rows, frames, sources, pri...]
    ppermute x4 -> x9, waiting for transfers between devices: 6.45 us -> 33.9 us  [the longest x7 32.9 us: body(): lax.ppermute(packed[k], 'frame', [(i, i ^ k) for i in range(peers)])]
    unnamed x31 -> x14, local copies, waits for them, and re-layouts: 22.5 us -> 0.03 us
    all_to_all x1 -> x0, local copies, waits for them, and re-layouts: 4.01 us -> none  [body(): lax.all_to_all(movie, 'frame', split_axis=2, concat_axis=0, tiled=True)]
    sub x1 -> x0, other arithmetic: 3.71 us -> none  [body(): return lag_products(raw_values - pixel_mean, rows, columns) / frames_total]
    slice x4 -> x16, local copies, waits for them, and re-layouts: 4.01 us -> 1.43 us  [the longest x8 0.72 us: edge_blocks(): first = [packed[t * size:t * size + PAIR] for t in range(tiles)]]
  transfers between devices with their start and end apart: 4 -> 9, of which waited for: 2 -> 7; matrix products, arithmetic and copies ran while one was open for 1% -> 3% of each run, Pallas kernels for 0% -> 9%
where the time goes in v1:
time: 89 us; the launch traced here: 88.1 us
  Pallas kernels  36.6 us (41%)
  waiting for transfers between devices  33.9 us (38%)
  starting transfers between devices  13.8 us (16%)
  local copies, waits for them, and re-layouts  2.76 us (3%)
    ppermute x7, waiting for transfers between devices, body(): lax.ppermute(packed[k], 'frame', [(i, i ^ k) for i in range(peers)])  32.9 us
    pallas_call x2, Pallas kernels, lag_sums(): pl.pallas_call(lambda *refs: lag_kernel(tiles, rows, frames, sources, pri...  25.2 us
    pallas_call x1, Pallas kernels, pack_rest(): pl.pallas_call(kernel, out_shape=[jax.ShapeDtypeStruct((length, LANES), j...  7.78 us
    ppermute x7, starting transfers between devices, body(): lax.ppermute(packed[k], 'frame', [(i, i ^ k) for i in range(peers)])  6.15 us
    ppermute x1, starting transfers between devices, exchange_rows(): lax.ppermute(jnp.stack([first for first, _ in pairs]), 'strip', down)  4.58 us
    pallas_call x1, Pallas kernels, pack_one(): pl.pallas_call(lambda *refs: pack_one_kernel(tiles, *refs), out_shape=jax...  3.66 us
    ppermute x1, starting transfers between devices, exchange_rows(): above = lax.ppermute(jnp.stack([last for _, last in pairs]), 'strip', up)  3.05 us
  transfers between devices with their start and end apart: 9, of which 7 were waited for; matrix products, arithmetic and copies ran while one was open for 3% of the time, Pallas kernels for 9%

profile of v1, /device:TPU:11, one launch (start us, length us, event | category | flops | bytes accessed | tf_op | source)
XLA Modules:
  0.0 88.1 jit_solution(15262068692468066633)
XLA Ops:
  0.0 0.7 pad_add_fusion.refs_0_
  0.7 3.7 %pack_one.1 = bf16[1040,128]{1,0:T(8,128)(2,1)} custom-call(s32[2]{0:T(128)} %pad_add_fusion.refs_0_, bf16[8,64,2048]{2,1,0:T(8,128)(2,1)} %refs_3_.1, bf16[8,64,2048]{2,1,0:T(8,128)(2,1)} %refs_3_.1, bf16[8,64,2048]{2,1,0:T(8,128)(2,1)} %refs_3_.1), custom_call_target="tpu_custom_call" | custom-call | tf_op jit(solution)/shard_map/pack_one/pallas_call | solution.py:93
  4.3 2.3 %collective-permute-start = (bf16[1040,128]{1,0:T(8,128)(2,1)}, bf16[1040,128]{1,0:T(8,128)(2,1)S(1)}, u32[]{:S(2)}, u32[]{:S(2)}) collective-permute-start(bf16[1040,128]{1,0:T(8,128)(2,1)} %pack_one.1), channel_id=1, source_target_pairs={{0,16},{4,20},{8,24},{12,28},{16,0},{20,4},{24,8},{28,12},{1,17},{... | collective-permute-start | bytes 798728 | tf_op jit(solution)/shard_map/ppermute | solution.py:457
  6.6 7.8 %pack_rest.1 = (bf16[1040,128]{1,0:T(8,128)(2,1)}, bf16[1040,128]{1,0:T(8,128)(2,1)}, bf16[1040,128]{1,0:T(8,128)(2,1)}, bf16[1040,128]{1,0:T(8,128)(2,1)}, bf16...) custom-call(s32[1]{0:T(128)} %bitcast.me_ref, bf16[8,64,2048]{2,1,0:T(8,128)(2,1)} %refs_3_.1), custom_call_target="tpu_custom_call" | custom-call | tf_op jit(solution)/shard_map/pack_rest/pallas_call | solution.py:151
  14.4 0.3 collective-permute-start.1
  14.7 0.2 collective-permute-start.2
  14.8 2.2 %collective-permute-start.3 = (bf16[1040,128]{1,0:T(8,128)(2,1)}, bf16[1040,128]{1,0:T(8,128)(2,1)S(1)}, u32[]{:S(2)}, u32[]{:S(2)}) collective-permute-start(bf16[1040,128]{1,0:T(8,128)(2,1)} %get-tuple-element.17), channel_id=1, source_target_pairs={{0,12},{4,8},{8,4},{12,0},{16,28},{20,24},{24,20},{28,16},{1,13},{... | collective-permute-start | bytes 798728 | tf_op jit(solution)/shard_map/ppermute | solution.py:457
  17.1 0.0 collective-permute-start.4
  17.1 0.7 slice.177
  17.8 0.7 fusion.7
  18.5 0.2 collective-permute-done.refs_6_
  18.7 0.0 copy-start.4
  18.7 1.2 %collective-permute-start.5 = (bf16[1040,128]{1,0:T(8,128)(2,1)}, bf16[1040,128]{1,0:T(8,128)(2,1)S(1)}, u32[]{:S(2)}, u32[]{:S(2)}) collective-permute-start(bf16[1040,128]{1,0:T(8,128)(2,1)} %get-tuple-element.19), channel_id=1, source_target_pairs={{0,24},{4,28},{8,16},{12,20},{16,8},{20,12},{24,0},{28,4},{1,25},{... | collective-permute-start | bytes 798728 | tf_op jit(solution)/shard_map/ppermute | solution.py:457
  19.9 1.7 %collective-permute-done.1.refs_9_ = bf16[1040,128]{1,0:T(8,128)(2,1)S(1)} collective-permute-done((bf16[1040,128]{1,0:T(8,128)(2,1)}, bf16[1040,128]{1,0:T(8,128)(2,1)S(1)}, u32[]{:S(2)}, u32[]{:S(2)}) %collective-permute-start.1) | collective-permute-done | bytes 266272 | tf_op jit(solution)/shard_map/ppermute | solution.py:457
  21.6 0.0 copy-start.5
  21.6 0.0 collective-permute-start.6
  21.6 7.2 %collective-permute-done.2.refs_12_ = bf16[1040,128]{1,0:T(8,128)(2,1)S(1)} collective-permute-done((bf16[1040,128]{1,0:T(8,128)(2,1)}, bf16[1040,128]{1,0:T(8,128)(2,1)S(1)}, u32[]{:S(2)}, u32[]{:S(2)}) %collective-permute-start.2) | collective-permute-done | bytes 266272 | tf_op jit(solution)/shard_map/ppermute | solution.py:457
  28.8 0.0 copy-start.6
  28.8 17.3 %collective-permute-done.3.refs_3_ = bf16[1040,128]{1,0:T(8,128)(2,1)S(1)} collective-permute-done((bf16[1040,128]{1,0:T(8,128)(2,1)}, bf16[1040,128]{1,0:T(8,128)(2,1)S(1)}, u32[]{:S(2)}, u32[]{:S(2)}) %collective-permute-start.3) | collective-permute-done | bytes 266272 | tf_op jit(solution)/shard_map/ppermute | solution.py:457
  46.1 0.0 copy-start
  46.1 0.0 collective-permute-done.4.refs_6_
  46.1 0.0 copy-start.1
  46.1 0.0 collective-permute-done.5.refs_9_
  46.1 0.0 copy-start.2
  46.2 6.6 %collective-permute-done.6.refs_12_ = bf16[1040,128]{1,0:T(8,128)(2,1)S(1)} collective-permute-done((bf16[1040,128]{1,0:T(8,128)(2,1)}, bf16[1040,128]{1,0:T(8,128)(2,1)S(1)}, u32[]{:S(2)}, u32[]{:S(2)}) %collective-permute-start.6) | collective-permute-done | bytes 266272 | tf_op jit(solution)/shard_map/ppermute | solution.py:457
  52.8 0.0 copy-start.3
  52.8 4.6 %collective-permute-start.8 = (bf16[8,48,128]{2,1,0:T(8,128)(2,1)S(1)}, bf16[8,48,128]{2,1,0:T(8,128)(2,1)S(1)}, u32[]{:S(2)}, u32[]{:S(2)}) collective-permute-start(bf16[8,48,128]{2,1,0:T(8,128)(2,1)S(1)} %constant_dynamic-update-slice_fusion.8), channel_id=1, source_target_pairs={{1,0},{2,1},{3,2},{5,4},{6,5},{7,6},{9,8},{10,9},{11,10},{13,12},{... | collective-permute-start | bytes 294920 | tf_op jit(solution)/shard_map/ppermute | solution.py:439
  57.5 3.0 %collective-permute-start.7 = (bf16[8,48,128]{2,1,0:T(8,128)(2,1)S(1)}, bf16[8,48,128]{2,1,0:T(8,128)(2,1)S(1)}, u32[]{:S(2)}, u32[]{:S(2)}) collective-permute-start(bf16[8,48,128]{2,1,0:T(8,128)(2,1)S(1)} %constant_dynamic-update-slice_fusion), channel_id=1, source_target_pairs={{0,1},{1,2},{2,3},{4,5},{5,6},{6,7},{8,9},{9,10},{10,11},{12,13},{... | collective-permute-start | bytes 294920 | tf_op jit(solution)/shard_map/ppermute | solution.py:438
  60.6 0.2 collective-permute-done.8
  60.8 0.7 slice_bitcast_fusion
  61.4 0.8 collective-permute-done.7
  62.2 0.6 slice_bitcast_fusion.1
  62.9 0.0 copy-done.4
  62.9 0.0 copy-done.5
  62.9 0.0 copy-done.6
  62.9 11.8 %lag_sums.1 = (f32[13,3,72,128]{3,2,1,0:T(8,128)}, f32[3,80,128]{2,1,0:T(8,128)}) custom-call(bf16[1040,128]{1,0:T(8,128)(2,1)} %get-tuple-element.14.refs_0_.refs_3_, bf16[48,128]{1,0:T(8,128)(2,1)} %get-tuple-element.70.refs_1_.refs_4_, bf16[48,128]{1,0:T(8,128)(2,1)} %get-tuple-element.62.refs_2_.refs_5_, ...), custom_call_target="tpu_custom_call" | custom-call | tf_op jit(solution)/shard_map/lag_sums/pallas_call | solution.py:412
  74.7 0.0 copy-done
  74.7 0.0 copy-done.1
  74.7 0.0 copy-done.2
  74.7 0.0 copy-done.3
  74.7 13.4 %lag_maps.1 = f32[25,64,256]{2,1,0:T(8,128)} custom-call(bf16[1040,128]{1,0:T(8,128)(2,1)} %get-tuple-element.14.refs_0_.refs_3_, bf16[48,128]{1,0:T(8,128)(2,1)} %get-tuple-element.70.refs_1_.refs_4_, bf16[48,128]{1,0:T(8,128)(2,1)} %get-tuple-element.62.refs_2_.refs_5_, bf16[1040,128]{1,0:T(8,128)(2,1)} %copy-done, ...), custom_call_target="tpu_custom_call" | custom-call | tf_op jit(solution)/shard_map/lag_maps/pallas_call | solution.py:412
  (29 shorter events, 0.2 us)
Async XLA Ops:
  4.3 14.4 %collective-permute-start = (bf16[1040,128]{1,0:T(8,128)(2,1)}, bf16[1040,128]{1,0:T(8,128)(2,1)S(1)}, u32[]{:S(2)}, u32[]{:S(2)}) collective-permute-start(bf16[1040,128]{1,0:T(8,128)(2,1)} %pack_one.1), channel_id=1, source_target_pairs={{0,16},{4,20},{8,24},{12,28},{16,0},{20,4},{24,8},{28,12},{1,17},{... | collective-permute-start | bytes 798728 | tf_op jit(solution)/shard_map/ppermute | solution.py:457
  14.4 7.2 %collective-permute-start.1 = (bf16[1040,128]{1,0:T(8,128)(2,1)}, bf16[1040,128]{1,0:T(8,128)(2,1)S(1)}, u32[]{:S(2)}, u32[]{:S(2)}) collective-permute-start(bf16[1040,128]{1,0:T(8,128)(2,1)} %get-tuple-element.15), channel_id=1, source_target_pairs={{0,4},{4,0},{8,12},{12,8},{16,20},{20,16},{24,28},{28,24},{1,5},{5... | collective-permute-start | bytes 798728 | tf_op jit(solution)/shard_map/ppermute | solution.py:457
  14.7 14.1 %collective-permute-start.2 = (bf16[1040,128]{1,0:T(8,128)(2,1)}, bf16[1040,128]{1,0:T(8,128)(2,1)S(1)}, u32[]{:S(2)}, u32[]{:S(2)}) collective-permute-start(bf16[1040,128]{1,0:T(8,128)(2,1)} %get-tuple-element.16), channel_id=1, source_target_pairs={{0,8},{4,12},{8,0},{12,4},{16,24},{20,28},{24,16},{28,20},{1,9},{5... | collective-permute-start | bytes 798728 | tf_op jit(solution)/shard_map/ppermute | solution.py:457
  14.8 31.2 %collective-permute-start.3 = (bf16[1040,128]{1,0:T(8,128)(2,1)}, bf16[1040,128]{1,0:T(8,128)(2,1)S(1)}, u32[]{:S(2)}, u32[]{:S(2)}) collective-permute-start(bf16[1040,128]{1,0:T(8,128)(2,1)} %get-tuple-element.17), channel_id=1, source_target_pairs={{0,12},{4,8},{8,4},{12,0},{16,28},{20,24},{24,20},{28,16},{1,13},{... | collective-permute-start | bytes 798728 | tf_op jit(solution)/shard_map/ppermute | solution.py:457
  17.1 29.0 %collective-permute-start.4 = (bf16[1040,128]{1,0:T(8,128)(2,1)}, bf16[1040,128]{1,0:T(8,128)(2,1)S(1)}, u32[]{:S(2)}, u32[]{:S(2)}) collective-permute-start(bf16[1040,128]{1,0:T(8,128)(2,1)} %get-tuple-element.18), channel_id=1, source_target_pairs={{0,20},{4,16},{8,28},{12,24},{16,4},{20,0},{24,12},{28,8},{1,21},{... | collective-permute-start | bytes 798728 | tf_op jit(solution)/shard_map/ppermute | solution.py:457
  18.7 44.2 %copy-start.4 = (bf16[1040,128]{1,0:T(8,128)(2,1)}, bf16[1040,128]{1,0:T(8,128)(2,1)S(1)}, u32[]{:S(2)}) copy-start(bf16[1040,128]{1,0:T(8,128)(2,1)S(1)} %collective-permute-done.refs_6_) | copy-start | bytes 798724
  18.7 27.4 %collective-permute-start.5 = (bf16[1040,128]{1,0:T(8,128)(2,1)}, bf16[1040,128]{1,0:T(8,128)(2,1)S(1)}, u32[]{:S(2)}, u32[]{:S(2)}) collective-permute-start(bf16[1040,128]{1,0:T(8,128)(2,1)} %get-tuple-element.19), channel_id=1, source_target_pairs={{0,24},{4,28},{8,16},{12,20},{16,8},{20,12},{24,0},{28,4},{1,25},{... | collective-permute-start | bytes 798728 | tf_op jit(solution)/shard_map/ppermute | solution.py:457
  21.6 41.3 %copy-start.5 = (bf16[1040,128]{1,0:T(8,128)(2,1)}, bf16[1040,128]{1,0:T(8,128)(2,1)S(1)}, u32[]{:S(2)}) copy-start(bf16[1040,128]{1,0:T(8,128)(2,1)S(1)} %collective-permute-done.1.refs_9_) | copy-start | bytes 798724
  21.6 31.2 %collective-permute-start.6 = (bf16[1040,128]{1,0:T(8,128)(2,1)}, bf16[1040,128]{1,0:T(8,128)(2,1)S(1)}, u32[]{:S(2)}, u32[]{:S(2)}) collective-permute-start(bf16[1040,128]{1,0:T(8,128)(2,1)} %get-tuple-element.20), channel_id=1, source_target_pairs={{0,28},{4,24},{8,20},{12,16},{16,12},{20,8},{24,4},{28,0},{1,29},{... | collective-permute-start | bytes 798728 | tf_op jit(solution)/shard_map/ppermute | solution.py:457
  28.8 34.1 %copy-start.6 = (bf16[1040,128]{1,0:T(8,128)(2,1)}, bf16[1040,128]{1,0:T(8,128)(2,1)S(1)}, u32[]{:S(2)}) copy-start(bf16[1040,128]{1,0:T(8,128)(2,1)S(1)} %collective-permute-done.2.refs_12_) | copy-start | bytes 798724
  46.1 28.6 %copy-start = (bf16[1040,128]{1,0:T(8,128)(2,1)}, bf16[1040,128]{1,0:T(8,128)(2,1)S(1)}, u32[]{:S(2)}) copy-start(bf16[1040,128]{1,0:T(8,128)(2,1)S(1)} %collective-permute-done.3.refs_3_) | copy-start | bytes 798724
  46.1 28.6 %copy-start.1 = (bf16[1040,128]{1,0:T(8,128)(2,1)}, bf16[1040,128]{1,0:T(8,128)(2,1)S(1)}, u32[]{:S(2)}) copy-start(bf16[1040,128]{1,0:T(8,128)(2,1)S(1)} %collective-permute-done.4.refs_6_) | copy-start | bytes 798724
  46.1 28.5 %copy-start.2 = (bf16[1040,128]{1,0:T(8,128)(2,1)}, bf16[1040,128]{1,0:T(8,128)(2,1)S(1)}, u32[]{:S(2)}) copy-start(bf16[1040,128]{1,0:T(8,128)(2,1)S(1)} %collective-permute-done.5.refs_9_) | copy-start | bytes 798724
  52.8 21.9 %copy-start.3 = (bf16[1040,128]{1,0:T(8,128)(2,1)}, bf16[1040,128]{1,0:T(8,128)(2,1)S(1)}, u32[]{:S(2)}) copy-start(bf16[1040,128]{1,0:T(8,128)(2,1)S(1)} %collective-permute-done.6.refs_12_) | copy-start | bytes 798724
  52.8 8.0 %collective-permute-start.8 = (bf16[8,48,128]{2,1,0:T(8,128)(2,1)S(1)}, bf16[8,48,128]{2,1,0:T(8,128)(2,1)S(1)}, u32[]{:S(2)}, u32[]{:S(2)}) collective-permute-start(bf16[8,48,128]{2,1,0:T(8,128)(2,1)S(1)} %constant_dynamic-update-slice_fusion.8), channel_id=1, source_target_pairs={{1,0},{2,1},{3,2},{5,4},{6,5},{7,6},{9,8},{10,9},{11,10},{13,12},{... | collective-permute-start | bytes 294920 | tf_op jit(solution)/shard_map/ppermute | solution.py:439
  57.5 4.7 %collective-permute-start.7 = (bf16[8,48,128]{2,1,0:T(8,128)(2,1)S(1)}, bf16[8,48,128]{2,1,0:T(8,128)(2,1)S(1)}, u32[]{:S(2)}, u32[]{:S(2)}) collective-permute-start(bf16[8,48,128]{2,1,0:T(8,128)(2,1)S(1)} %constant_dynamic-update-slice_fusion), channel_id=1, source_target_pairs={{0,1},{1,2},{2,3},{4,5},{5,6},{6,7},{8,9},{9,10},{10,11},{12,13},{... | collective-permute-start | bytes 294920 | tf_op jit(solution)/shard_map/ppermute | solution.py:438

commit v2 on v0

v2 whole, which is shorter than its diff:
```python
import math

import jax
import jax.numpy as jnp
from jax import lax
from jax.experimental import pallas as pl
from jax.experimental.pallas import tpu as pltpu
from jax.sharding import PartitionSpec as P

REACH = 2
LANES = 128
GROUP = 8
FOLD = LANES // (2 * REACH)
PAD = 2 * REACH
PAIR = 2 * GROUP
LAG_LIST = tuple(
    (a, b)
    for a in range(REACH + 1)
    for b in range(-REACH, REACH + 1)
    if a > 0 or b >= 0
)
def cost(micros):
    work = int(micros * 1e9 * 0.3)
    return pl.CostEstimate(flops=work, bytes_accessed=work // 300, transcendentals=0)


VMEM = 56 * 1024 * 1024


def shifted(ring, index, offset):
    tile = ring[index]
    if offset == 0:
        return tile
    lane = lax.broadcasted_iota(jnp.int32, tile.shape, tile.ndim - 1)
    if offset > 0:
        other = ring[(index + 1) % len(ring)]
        mixed = jnp.where(lane < offset, other, tile)
    else:
        other = ring[index - 1]
        mixed = jnp.where(lane >= LANES + offset, other, tile)
    return pltpu.roll(mixed, (-offset) % LANES, 1)


def folded_pairs(pairs):
    return -(-pairs // FOLD)


def both_rows(ref, index, row, stride):
    return jnp.concatenate(
        [ref[index, pl.ds(row + j, GROUP, stride=stride), :] for j in range(2)], axis=0
    )


def lay_out(ref, place, value, above=None, below=None):
    frames, rows, _ = value.shape
    for f in range(frames):
        start = f * (rows + PAD)
        ref[place, start + REACH : start + REACH + rows, :] = value[f].astype(jnp.float32)
        if above is not None:
            ref[place, start : start + REACH, :] = above[f].astype(jnp.float32)
            end = start + REACH + rows
            ref[place, end : end + REACH, :] = below[f].astype(jnp.float32)


def edge_sides(ref, left, right, row, stride):
    lane = lax.broadcasted_iota(jnp.int32, (PAIR, LANES), 1)
    return jnp.where(
        lane >= LANES - REACH,
        both_rows(ref, left, row, stride),
        both_rows(ref, right, row, stride),
    )


def folded_in(edge, sides, index):
    lane = lax.broadcasted_iota(jnp.int32, (PAIR, LANES), 1)
    first = 2 * REACH * index
    placed = pltpu.roll(sides, first + REACH, 1)
    return jnp.where((lane >= first) & (lane < first + 2 * REACH), placed, edge)


def write_packed(ref, places, rows, offset, outs):
    stride = rows + PAD
    pairs = outs_pairs = rows // 2 + (2 if offset == 0 else 0)
    span = pairs * PAIR
    zero = jnp.zeros((PAIR, LANES), jnp.float32)
    for part in range(folded_pairs(pairs)):

        def pair(q, edges, part=part):
            row = offset + 2 * q
            result = []
            for (own, left, right), out, edge in zip(places, outs, edges):
                for t, place in enumerate(own):
                    start = pl.multiple_of(t * span + q * PAIR, PAIR)
                    both = both_rows(ref, place, row, stride)
                    out[pl.ds(start, PAIR), :] = both.astype(jnp.bfloat16)
                sides = edge_sides(ref, left, right, row, stride)
                result.append(folded_in(edge, sides, q - part * FOLD))
            return tuple(result)

        first, last = part * FOLD, min((part + 1) * FOLD, outs_pairs)
        unroll = 4 if (last - first) % 4 == 0 else 1
        edges = lax.fori_loop(first, last, pair, (zero,) * len(outs), unroll=unroll)
        for (own, _, _), out, edge in zip(places, outs, edges):
            start = len(own) * span + part * PAIR
            out[start : start + PAIR, :] = edge.astype(jnp.bfloat16)


def pack_one_kernel(tiles, block_ref, main_ref, left_ref, right_ref, out_ref, values):
    rows = main_ref.shape[1]
    block, blocks = block_ref[0], block_ref[1]
    for t in range(tiles):
        lay_out(values, t, main_ref[:, :, t * LANES : (t + 1) * LANES])
    lay_out(values, tiles, left_ref[...])
    lay_out(values, tiles + 1, right_ref[...])

    @pl.when(block == 0)
    def _():
        values[tiles] = jnp.zeros(values.shape[1:], jnp.float32)

    @pl.when(block == blocks - 1)
    def _():
        values[tiles + 1] = jnp.zeros(values.shape[1:], jnp.float32)

    places = [(list(range(tiles)), tiles, tiles + 1)]
    write_packed(values, places, rows, REACH, [out_ref])


def packed_length(rows, tiles):
    return tiles * rows * GROUP + folded_pairs(rows // 2) * PAIR


def pack_one(movie, block, blocks):
    frames, rows, width = movie.shape
    columns = width // blocks
    tiles = columns // LANES
    last = width // LANES - 1
    length = packed_length(rows, tiles)
    return pl.pallas_call(
        lambda *refs: pack_one_kernel(tiles, *refs),
        out_shape=jax.ShapeDtypeStruct((length, LANES), jnp.bfloat16),
        grid_spec=pltpu.PrefetchScalarGridSpec(
            num_scalar_prefetch=1,
            grid=(1,),
            in_specs=[
                pl.BlockSpec((frames, rows, columns), lambda i, s: (0, 0, s[0])),
                pl.BlockSpec(
                    (frames, rows, LANES),
                    lambda i, s: (0, 0, jnp.maximum(s[0] * tiles - 1, 0)),
                ),
                pl.BlockSpec(
                    (frames, rows, LANES),
                    lambda i, s: (0, 0, jnp.minimum(s[0] * tiles + tiles, last)),
                ),
            ],
            out_specs=pl.BlockSpec((length, LANES), lambda i, s: (0, 0)),
            scratch_shapes=[
                pltpu.VMEM((tiles + 2, frames * (rows + PAD), LANES), jnp.float32)
            ],
        ),
        compiler_params=pltpu.CompilerParams(vmem_limit_bytes=VMEM),
        name="pack_one",
        cost_estimate=cost(3),
    )(jnp.stack([block, jnp.int32(blocks)]), movie, movie, movie)


def pack_kernel(tiles, skip, me_ref, movie_ref, above_ref, below_ref, *refs):
    outs, rest, pivot, values = list(refs[:-3]), refs[-3], refs[-2], refs[-1]
    frames, rows, width = movie_ref.shape
    stride = rows + PAD
    count = width // LANES
    blocks = count // tiles
    zero = jnp.zeros((frames * stride, LANES), jnp.float32)
    values[0] = zero
    values[count + 1] = zero
    for t in range(count):
        lanes = slice(t * LANES, (t + 1) * LANES)
        lay_out(
            values,
            t + 1,
            movie_ref[:, :, lanes],
            above_ref[:, :, lanes],
            below_ref[:, :, lanes],
        )
    places = []
    for k in range(blocks):
        first = 1 + (me_ref[0] ^ k) * tiles
        places.append(([first + t for t in range(tiles)], first - 1, first + tiles))
    kept = [k for k in range(blocks) if k != skip]
    write_packed(values, [places[k] for k in kept], rows, 0, outs)

    own, left, right = places[skip]
    edge = jnp.zeros((PAIR, LANES), jnp.float32)
    for n, row in enumerate((0, rows + REACH)):
        for t, place in enumerate(own):
            both = both_rows(values, place, row, stride)
            start = (t * 2 + n) * PAIR
            rest[start : start + PAIR, :] = both.astype(jnp.bfloat16)
        edge = folded_in(edge, edge_sides(values, left, right, row, stride), n)
    rest[tiles * 2 * PAIR :, :] = edge.astype(jnp.bfloat16)

    own, left, right = places[0]
    lane = lax.broadcasted_iota(jnp.int32, (PAIR, LANES), 1)

    def first_frame(place, row):
        parts = [
            jnp.broadcast_to(values[place, pl.ds(row + j, 1), :], (GROUP, LANES))
            for j in range(2)
        ]
        return jnp.concatenate(parts, axis=0)

    def pair(q, carry):
        at = pl.ds(pl.multiple_of(q * PAIR, PAIR), PAIR)
        for t, place in enumerate(own):
            pivot[t, at, :] = first_frame(place, 2 * q).astype(jnp.bfloat16)
        sides = jnp.where(
            lane >= LANES - REACH, first_frame(left, 2 * q), first_frame(right, 2 * q)
        )
        pivot[tiles, at, :] = sides.astype(jnp.bfloat16)
        return carry

    lax.fori_loop(0, rows // 2 + 2, pair, 0, unroll=2)


def pack_rest(movie, above, below, me, blocks, skip):
    frames, rows, width = movie.shape
    tiles = width // blocks // LANES
    length = tiles * (rows + 2 * REACH) * GROUP + folded_pairs(rows // 2 + 2) * PAIR
    whole = pl.BlockSpec(memory_space=pltpu.VMEM)
    kept = [k for k in range(blocks) if k != skip]
    shapes = [(length, LANES)] * len(kept)
    shapes += [((tiles * 2 + 1) * PAIR, LANES)]
    shapes += [(tiles + 1, (rows + 2 * REACH) * GROUP, LANES)]
    results = pl.pallas_call(
        lambda *refs: pack_kernel(tiles, skip, *refs),
        out_shape=[jax.ShapeDtypeStruct(shape, jnp.bfloat16) for shape in shapes],
        in_specs=[pl.BlockSpec(memory_space=pltpu.SMEM)] + [whole] * 3,
        out_specs=[whole] * len(shapes),
        scratch_shapes=[
            pltpu.VMEM((width // LANES + 2, frames * (rows + PAD), LANES), jnp.float32)
        ],
        compiler_params=pltpu.CompilerParams(vmem_limit_bytes=VMEM),
        name="pack_rest",
        cost_estimate=cost(5),
    )(me[None], movie, above, below)
    return dict(zip(kept, results)), results[-2], results[-1]


def unfolded(edge, index):
    shift = 2 * LANES - 2 * REACH * index - REACH
    return pltpu.roll(edge, lax.rem(shift, LANES), 1)


def unfold_edges(tiles, rows, block, edges, i):
    pairs = rows // 2 + 2

    def put(q, edge, index):
        start = q * PAIR
        if not isinstance(start, int):
            start = pl.multiple_of(start, PAIR)
        edges[i, pl.ds(start, PAIR), :] = unfolded(edge, index).astype(jnp.bfloat16)

    def tile_of(ref, start):
        return ref[start : start + PAIR, :].astype(jnp.float32)

    body = block[0]
    if len(block) > 1:
        around = tile_of(block[1], tiles * 2 * PAIR)
        put(0, around, 0)
        put(pairs - 1, around, 1)
        pairs, lead = rows // 2, 1
    else:
        lead = 0
    for part in range(folded_pairs(pairs)):
        edge = tile_of(body, (tiles * pairs + part) * PAIR)

        def fill(q, carry, part=part, edge=edge):
            put(q + lead, edge, q - part * FOLD)
            return carry

        first, last = part * FOLD, min((part + 1) * FOLD, pairs)
        unroll = 8 if (last - first) % 8 == 0 else 1
        lax.fori_loop(first, last, fill, 0, unroll=unroll)


def merged(first, second, distance):
    row = lax.broadcasted_iota(jnp.int32, first.shape, 0)
    low = (row & distance) == 0
    kept = jnp.where(low, first, second)
    moved = jnp.where(low, second, first)
    return kept + pltpu.roll(moved, GROUP - distance, 0)


def lag_kernel(tiles, rows, frames, counts, has_prior, last, *refs):
    refs = list(refs)
    pivot_ref = refs[0]
    refs = refs[1:]
    sources = len(counts)
    blocks = []
    for count in counts:
        blocks.append(refs[:count])
        refs = refs[count:]
    prior = None
    if has_prior:
        prior, prior_sum = refs[:2]
        refs = refs[2:]
    if last:
        out, edges, rings, shifts, staged, sums, means, cov, sems = refs
    else:
        maps, sums, edges, rings, shifts = refs
    ring = tiles + 1
    span = (rows + 2 * REACH) * GROUP

    for i, block in enumerate(blocks):
        unfold_edges(tiles, rows, block, edges, i)
        if len(block) > 1:
            body, around = block
            for t in range(tiles):
                start = t * rows * GROUP
                rings[t, PAIR : span - PAIR, :] = body[start : start + rows * GROUP, :]
                start = t * 2 * PAIR
                rings[t, :PAIR, :] = around[start : start + PAIR, :]
                rings[t, span - PAIR :, :] = around[start + PAIR : start + 2 * PAIR, :]

    def raw_values(i, t, start, size):
        if t == tiles:
            return edges[i, pl.ds(start, size), :]
        if len(blocks[i]) > 1:
            return rings[t, pl.ds(start, size), :]
        start = pl.multiple_of(t * span + start, PAIR)
        return blocks[i][0][pl.ds(start, size), :]

    source = lax.broadcasted_iota(jnp.int32, (2 * LANES, LANES), 0)
    target = lax.broadcasted_iota(jnp.int32, (2 * LANES, LANES), 1)
    moves = jnp.concatenate(
        [jnp.where(source == target + b, 1.0, 0.0) for b in range(1, REACH + 1)], axis=1
    ).astype(jnp.bfloat16)
    size = span // (2 if sources < 3 else 17)
    if size % PAIR or span % size:
        size = PAIR

    def spread(c, carry):
        start = pl.multiple_of(c * size, PAIR)
        at = pl.ds(start, size)
        raw = [[pivot_ref[t, at, :] for t in range(ring)]]
        for i in range(sources):
            raw.append([raw_values(i, t, start, size) for t in range(ring)])
        wide = jnp.concatenate(
            [
                jnp.concatenate([r[t], r[(t + 1) % ring]], axis=1)
                for r in raw
                for t in range(ring)
            ],
            axis=0,
        )
        moved = jnp.dot(wide, moves, preferred_element_type=jnp.float32)

        def version(i, t, b):
            if b == 0:
                return raw[i][t].astype(jnp.float32)
            first = (i * ring + t) * size
            return moved[first : first + size, (b - 1) * LANES : b * LANES]

        for t in range(ring):
            for b in range(REACH + 1):
                pivot = version(0, t, b)
                for i in range(1, sources + 1):
                    shifts[b, i - 1, t, at, :] = version(i, t, b) - pivot
        return carry

    lax.fori_loop(0, span // size, spread, 0)

    def value(i, t, slot, b):
        start = slot * GROUP
        if not isinstance(start, int):
            start = pl.multiple_of(start, GROUP)
        return shifts[b, i, t, pl.ds(start, GROUP), :]

    def over_blocks(term):
        total = term(0)
        for i in range(1, sources):
            total = total + term(i)
        return total

    def fold_rows(parts):
        distance = 1
        while len(parts) > 1:
            parts = [merged(x, y, distance) for x, y in zip(parts[::2], parts[1::2])]
            distance *= 2
        return parts[0]

    def fold_two(first, second):
        total = merged(first, second, 1)
        total = total + pltpu.roll(total, GROUP - 2, 0)
        return total + pltpu.roll(total, GROUP // 2, 0)

    for t in range(ring):

        def put_sum(at, total, t=t):
            if has_prior:
                total = total + prior_sum[t, at, :]
            sums[t, at, :] = total

        def row_sum(slot, t=t):
            return over_blocks(lambda i: value(i, t, slot, 0))

        put_sum(slice(0, GROUP), fold_two(row_sum(0), row_sum(1)))
        put_sum(
            slice(rows + GROUP, rows + 2 * GROUP),
            fold_two(row_sum(rows + REACH), row_sum(rows + REACH + 1)),
        )

        def sum_rows(g, carry, t=t):
            total = fold_rows([row_sum(g * GROUP + REACH + j) for j in range(GROUP)])
            put_sum(pl.ds(pl.multiple_of((g + 1) * GROUP, GROUP), GROUP), total)
            return carry

        lax.fori_loop(0, rows // GROUP, sum_rows, 0, unroll=2)

    scale = 1.0 / frames
    sublane = lax.broadcasted_iota(jnp.int32, (GROUP, LANES), 0)
    if last:

        def spread_sums(g, carry):
            at = pl.ds(pl.multiple_of(g * GROUP, GROUP), GROUP)
            after = pl.ds(pl.multiple_of((g + 1) * GROUP, GROUP), GROUP)
            for a in range(REACH + 1):
                row_ring = [sums[t, at, :] for t in range(ring)]
                if a > 0:
                    row_ring = [
                        pltpu.roll(
                            jnp.where(sublane < a, sums[t, after, :], row), GROUP - a, 0
                        )
                        for t, row in enumerate(row_ring)
                    ]
                for t in range(ring):
                    for b in range(REACH + 1):
                        means[a, b, t, at, :] = shifted(row_ring, t, b)
            return carry

        lax.fori_loop(0, rows // GROUP + 1, spread_sums, 0)

    def put_map(k, t, at, total):
        a, b = LAG_LIST[k]
        if has_prior:
            total = total + prior[k, t, at, :]
        if last:
            here, there = means[0, max(-b, 0), t, at, :], means[a, max(b, 0), t, at, :]
            cov[k, t, at, :] = (total - here * scale * there) * scale
        else:
            maps[k, t, at, :] = total

    half = GROUP // 2
    wanted = [
        [k for k, (a, b) in enumerate(LAG_LIST) if t < tiles or b != 0]
        for t in range(ring)
    ]

    def product(i, t, slot, k):
        a, b = LAG_LIST[k]
        return value(i, t, slot, max(-b, 0)) * value(i, t, slot + a, max(b, 0))

    for t in range(ring):
        for k in wanted[t]:
            if LAG_LIST[k][0] > 0:
                first, second = [
                    over_blocks(lambda i, j=j: product(i, t, j, k)) for j in range(2)
                ]
                put_map(k, t, slice(0, GROUP), fold_two(first, second))

    def products(t, g):
        at = pl.ds(pl.multiple_of((g + 1) * GROUP, GROUP), GROUP)
        for a in range(REACH + 1):
            chosen = [k for k in wanted[t] if LAG_LIST[k][0] == a]
            folds = {k: [] for k in chosen}
            for h in range(2):
                slots = [g * GROUP + REACH + h * half + j for j in range(half)]
                totals = {k: [None] * half for k in chosen}
                for i in range(sources):
                    for k in chosen:
                        for j, slot in enumerate(slots):
                            part = product(i, t, slot, k)
                            if i > 0:
                                part = totals[k][j] + part
                            totals[k][j] = part
                for k in chosen:
                    x = merged(totals[k][0], totals[k][1], 1)
                    y = merged(totals[k][2], totals[k][3], 1)
                    folds[k].append(merged(x, y, 2))
            for k in chosen:
                put_map(k, t, at, merged(folds[k][0], folds[k][1], 4))

    def place(g):
        return pl.ds(pl.multiple_of(g * GROUP, GROUP), GROUP)

    def write(g):
        side = 2 * REACH + 1
        for k, (a, b) in enumerate(LAG_LIST):
            index = side * (a + REACH) + b + REACH
            mirror = side**2 - 1 - index
            for n, rise, offset in ((index, 0, min(b, 0)), (mirror, a, min(-b, 0))):
                row_ring = [
                    cov[k, t, place(g + 1), :] if t < tiles or offset else None
                    for t in range(ring)
                ]
                if rise > 0:
                    row_ring = [
                        row
                        if row is None
                        else pltpu.roll(
                            jnp.where(
                                sublane >= GROUP - rise, cov[k, t, place(g), :], row
                            ),
                            rise,
                            0,
                        )
                        for t, row in enumerate(row_ring)
                    ]
                for t in range(tiles):
                    lanes = slice(t * LANES, (t + 1) * LANES)
                    staged[n, place(g), lanes] = shifted(row_ring, t, offset)
                if index == mirror:
                    break

    def copy_out(g):
        rows_of = place(g)
        return pltpu.make_async_copy(
            staged.at[:, rows_of, :], out.at[:, rows_of, :], sems.at[g]
        )

    half_groups = rows // GROUP // 2
    for first in (0, half_groups):

        def sum_eight(g, carry):
            for t in range(ring):
                products(t, g)
            return carry

        lax.fori_loop(first, first + half_groups, sum_eight, 0)
        if last:

            def write_eight(g, carry):
                write(g)
                copy_out(g).start()
                return carry

            lax.fori_loop(first, first + half_groups, write_eight, 0)
    if last:

        def finish(g, carry):
            copy_out(g).wait()
            return carry

        lax.fori_loop(0, rows // GROUP, finish, 0)


def room(*parts):
    total = 0
    for leaf in jax.tree.leaves(parts):
        if hasattr(leaf, "shape") and jnp.issubdtype(leaf.dtype, jnp.floating):
            total += math.prod(leaf.shape) * jnp.dtype(leaf.dtype).itemsize
    return total * 5 // 4 + 4 * 1024 * 1024


def lag_sums(pivot, blocks, rows, tiles, frames, prior=None, last=False):
    sources = len(blocks)
    counts = [len(block) for block in blocks]
    ring = tiles + 1
    span = (rows + 2 * REACH) * GROUP
    operands = [pivot] + [a for block in blocks for a in block] + list(prior or ())
    whole = pl.BlockSpec(memory_space=pltpu.VMEM)
    map_shape = (len(LAG_LIST), ring, rows + GROUP, LANES)
    sum_shape = (ring, rows + 2 * GROUP, LANES)
    scratch = [
        pltpu.VMEM((sources, span, LANES), jnp.bfloat16),
        pltpu.VMEM((tiles, span, LANES), jnp.bfloat16),
        pltpu.VMEM((REACH + 1, sources, ring, span, LANES), jnp.float32),
    ]
    if last:
        shape = ((2 * REACH + 1) ** 2, rows, tiles * LANES)
        out_shape = jax.ShapeDtypeStruct(shape, jnp.float32)
        out_specs = pl.BlockSpec(memory_space=pl.ANY)
        scratch += [
            pltpu.VMEM(shape, jnp.float32),
            pltpu.VMEM(sum_shape, jnp.float32),
            pltpu.VMEM((REACH + 1,) * 2 + (ring, rows + GROUP, LANES), jnp.float32),
            pltpu.VMEM(map_shape, jnp.float32),
            pltpu.SemaphoreType.DMA((rows // GROUP,)),
        ]
    else:
        out_shape = (
            jax.ShapeDtypeStruct(map_shape, jnp.float32),
            jax.ShapeDtypeStruct(sum_shape, jnp.float32),
        )
        out_specs = (whole, whole)
    return pl.pallas_call(
        lambda *refs: lag_kernel(
            tiles, rows, frames, counts, prior is not None, last, *refs
        ),
        out_shape=out_shape,
        in_specs=[whole] * len(operands),
        out_specs=out_specs,
        scratch_shapes=scratch,
        compiler_params=pltpu.CompilerParams(
            vmem_limit_bytes=room(scratch, operands, out_shape)
        ),
        name="lag_maps" if last else "lag_sums",
        cost_estimate=cost(2 + 2 * sources),
    )(*operands)


def body(movie):
    frames_here, rows, width = movie.shape
    peers = lax.axis_size("frame")
    tiles = width // peers // LANES
    me = lax.axis_index("frame")
    frames = frames_here * peers
    half = peers // 2
    far = list(range(half, peers))
    near = list(range(1, half))
    strips = lax.axis_size("strip")
    up = [(i, i + 1) for i in range(strips - 1)]
    down = [(j, i) for i, j in up]
    moved = {}

    def send(k, payload, after=None):
        if after is not None:
            payload, moved[after] = lax.optimization_barrier((payload, moved[after]))
        moved[k] = lax.ppermute(payload, "frame", [(i, i ^ k) for i in range(peers)])

    ahead = pack_one(movie, me ^ far[0], peers)
    send(far[0], ahead)
    last, initial = movie[:, rows - REACH :, :], movie[:, :REACH, :]
    above = lax.ppermute(last, "strip", up)
    below = lax.ppermute(initial, "strip", down)
    packed, rest, pivot = pack_rest(movie, above, below, me, peers, far[0])
    rest, moved[far[0]] = lax.optimization_barrier((rest, moved[far[0]]))
    around = lax.ppermute(rest, "frame", [(i, i ^ far[0]) for i in range(peers)])
    for k in far[1:2] + near:
        send(k, packed[k], far[0])
    for n, k in enumerate(far[2:]):
        send(k, packed[k], near[n % len(near)])

    def sums(group, prior=None, last=False):
        blocks = [(moved[k], around) if k == far[0] else (moved[k],) for k in group]
        return lag_sums(pivot, blocks, rows, tiles, frames, prior, last)

    moved[0] = packed[0]
    prior = sums([0] + far[:1] + near[:-1])
    prior = sums(near[-1:] + far[1:-2], prior)
    prior = sums(far[-2:-1], prior)
    return sums(far[-1:], prior, True)


def solution(mesh):
    return jax.shard_map(
        body,
        mesh=mesh,
        in_specs=(P("frame", "strip", None),),
        out_specs=P(None, "strip", "frame"),
        check_vma=False,
    )
```

time: 169 us -> 74.9 us (0.44)
  other arithmetic: 64.6 us -> 0.58 us
  blocking collectives: 50.7 us -> 0 us
  Pallas kernels: 0 us -> 30.4 us
  local copies, waits for them, and re-layouts: 32.7 us -> 3.71 us
  waiting for transfers between devices: 6.45 us -> 26.4 us
    reduce_sum x3 -> x0, other arithmetic: 58.1 us -> none  [the longest x2 53 us: lag_products(): products.append(jnp.sum(centre * shifted, axis=0))]
    all_to_all x1 -> x0, blocking collectives: 50.7 us -> none  [body(): lax.all_to_all(movie, 'frame', split_axis=2, concat_axis=0, tiled=True)]
    pallas_call x0 -> x6, Pallas kernels: none -> 30.4 us  [the longest x4 22 us: lag_sums(): pl.pallas_call(lambda *refs: lag_kernel(tiles, rows, frames, counts, prio...]
    ppermute x4 -> x10, waiting for transfers between devices: 6.45 us -> 26.4 us  [the longest x7 25.1 us: send(): lax.ppermute(payload, 'frame', [(i, i ^ k) for i in range(peers)])]
    unnamed x31 -> x8, local copies, waits for them, and re-layouts: 22.5 us -> 2.57 us
    all_to_all x1 -> x0, local copies, waits for them, and re-layouts: 4.01 us -> none  [body(): lax.all_to_all(movie, 'frame', split_axis=2, concat_axis=0, tiled=True)]
    sub x1 -> x0, other arithmetic: 3.71 us -> none  [body(): return lag_products(raw_values - pixel_mean, rows, columns) / frames_total]
    slice x4 -> x1, local copies, waits for them, and re-layouts: 4.01 us -> 1.13 us  [body(): last, initial = (movie[:, rows - REACH:, :], movie[:, :REACH, :])]
  transfers between devices with their start and end apart: 4 -> 10, of which waited for: 2 -> 5; matrix products, arithmetic and copies ran while one was open for 1% -> 2% of each run, Pallas kernels for 0% -> 29%
where the time goes in v2:
time: 74.9 us; the launch traced here: 74.3 us
  Pallas kernels  30.4 us (41%)
  waiting for transfers between devices  26.4 us (35%)
  starting transfers between devices  13.2 us (18%)
  local copies, waits for them, and re-layouts  3.71 us (5%)
    ppermute x7, waiting for transfers between devices, send(): lax.ppermute(payload, 'frame', [(i, i ^ k) for i in range(peers)])  25.1 us
    pallas_call x4, Pallas kernels, lag_sums(): pl.pallas_call(lambda *refs: lag_kernel(tiles, rows, frames, counts, prio...  22 us
    ppermute x7, starting transfers between devices, send(): lax.ppermute(payload, 'frame', [(i, i ^ k) for i in range(peers)])  6.56 us
    pallas_call x1, Pallas kernels, pack_rest(): pl.pallas_call(lambda *refs: pack_kernel(tiles, skip, *refs), out_shape=[...  5.14 us
    pallas_call x1, Pallas kernels, pack_one(): pl.pallas_call(lambda *refs: pack_one_kernel(tiles, *refs), out_shape=jax...  3.21 us
    ppermute x1, starting transfers between devices, body(): above = lax.ppermute(last, 'strip', up)  3.05 us
    ppermute x1, starting transfers between devices, body(): below = lax.ppermute(initial, 'strip', down)  2.86 us
    unnamed x8, local copies, waits for them, and re-layouts  2.57 us
  transfers between devices with their start and end apart: 10, of which 5 were waited for; matrix products, arithmetic and copies ran while one was open for 2% of the time, Pallas kernels for 29%

profile of v2, /device:TPU:11, one launch (start us, length us, event | category | flops | bytes accessed | tf_op | source)
XLA Modules:
  0.0 74.3 jit_solution(4215535511267929864)
XLA Ops:
  0.0 0.6 pad_add_fusion.refs_0_
  0.6 3.2 %pack_one.1 = bf16[1040,128]{1,0:T(8,128)(2,1)} custom-call(s32[2]{0:T(128)} %pad_add_fusion.refs_0_, bf16[8,64,2048]{2,1,0:T(8,128)(2,1)} %refs_3_.1, bf16[8,64,2048]{2,1,0:T(8,128)(2,1)} %refs_3_.1, bf16[8,64,2048]{2,1,0:T(8,128)(2,1)} %refs_3_.1), custom_call_target="tpu_custom_call" | custom-call | flops 900000000 | bytes 3000000 | tf_op jit(solution)/shard_map/pack_one/pallas_call | solution.py:138
  3.8 2.3 %collective-permute-start.2 = (bf16[1040,128]{1,0:T(8,128)(2,1)}, bf16[1040,128]{1,0:T(8,128)(2,1)S(1)}, u32[]{:S(2)}, u32[]{:S(2)}) collective-permute-start(bf16[1040,128]{1,0:T(8,128)(2,1)} %pack_one.1), channel_id=1, source_target_pairs={{0,16},{4,20},{8,24},{12,28},{16,0},{20,4},{24,8},{28,12},{1,17},{... | collective-permute-start | bytes 798728 | tf_op jit(solution)/shard_map/ppermute | solution.py:628
  6.1 1.1 %fusion = (bf16[8,2,2048]{2,1,0:T(2,128)(2,1)S(1)}, bf16[8,2,2048]{2,1,0:T(2,128)(2,1)S(1)}) fusion(bf16[8,64,2048]{2,1,0:T(8,128)(2,1)} %refs_3_.1), kind=kLoop, calls=%fused_computation.1 | loop fusion | bytes 262144 | tf_op jit(solution)/shard_map/slice | solution.py:632
  7.2 2.9 %collective-permute-start.1 = (bf16[8,2,2048]{2,1,0:T(2,128)(2,1)S(1)}, bf16[8,2,2048]{2,1,0:T(2,128)(2,1)S(1)}, u32[]{:S(2)}, u32[]{:S(2)}) collective-permute-start(bf16[8,2,2048]{2,1,0:T(2,128)(2,1)S(1)} %get-tuple-element.63), channel_id=1, source_target_pairs={{1,0},{2,1},{3,2},{5,4},{6,5},{7,6},{9,8},{10,9},{11,10},{13,12},{... | collective-permute-start | bytes 196616 | tf_op jit(solution)/shard_map/ppermute | solution.py:634
  10.1 3.0 %collective-permute-start = (bf16[8,2,2048]{2,1,0:T(2,128)(2,1)S(1)}, bf16[8,2,2048]{2,1,0:T(2,128)(2,1)S(1)}, u32[]{:S(2)}, u32[]{:S(2)}) collective-permute-start(bf16[8,2,2048]{2,1,0:T(2,128)(2,1)S(1)} %get-tuple-element.64), channel_id=1, source_target_pairs={{0,1},{1,2},{2,3},{4,5},{5,6},{6,7},{8,9},{9,10},{10,11},{12,13},{... | collective-permute-start | bytes 196616 | tf_op jit(solution)/shard_map/ppermute | solution.py:633
  13.1 0.2 collective-permute-done.1.refs_3_
  13.4 0.0 copy-start.2
  13.4 1.1 %collective-permute-done.refs_2_ = bf16[8,2,2048]{2,1,0:T(2,128)(2,1)S(1)} collective-permute-done((bf16[8,2,2048]{2,1,0:T(2,128)(2,1)S(1)}, bf16[8,2,2048]{2,1,0:T(2,128)(2,1)S(1)}, u32[]{:S(2)}, u32[]{:S(2)}) %collective-permute-start) | collective-permute-done | bytes 65568 | tf_op jit(solution)/shard_map/ppermute | solution.py:633
  14.5 0.0 copy-start.3
  14.5 0.0 copy-done.2
  14.5 0.6 copy-done.3
  15.1 5.1 %pack_rest.1 = (bf16[1120,128]{1,0:T(8,128)(2,1)}, bf16[1120,128]{1,0:T(8,128)(2,1)}, bf16[1120,128]{1,0:T(8,128)(2,1)}, bf16[1120,128]{1,0:T(8,128)(2,1)}, bf16...) custom-call(s32[1]{0:T(128)} %bitcast.refs_0_, ...), custom_call_target="tpu_custom_call" | custom-call | flops 1500000000 | bytes 5000000 | tf_op jit(solution)/shard_map/pack_rest/pallas_call | solution.py:233
  20.2 0.0 collective-permute-done.2.refs_2_
  20.2 0.2 collective-permute-start.3
  20.4 0.3 collective-permute-start.5
  20.7 0.7 collective-permute-start.9
  21.4 2.4 %collective-permute-start.7 = (bf16[1120,128]{1,0:T(8,128)(2,1)}, bf16[1120,128]{1,0:T(8,128)(2,1)S(1)}, u32[]{:S(2)}, u32[]{:S(2)}) collective-permute-start(bf16[1120,128]{1,0:T(8,128)(2,1)} %get-tuple-element.50), channel_id=1, source_target_pairs={{0,12},{4,8},{8,4},{12,0},{16,28},{20,24},{24,20},{28,16},{1,13},{... | collective-permute-start | bytes 860168 | tf_op jit(solution)/shard_map/ppermute | solution.py:628
  23.8 1.4 %collective-permute-start.8 = (bf16[1120,128]{1,0:T(8,128)(2,1)}, bf16[1120,128]{1,0:T(8,128)(2,1)S(1)}, u32[]{:S(2)}, u32[]{:S(2)}) collective-permute-start(bf16[1120,128]{1,0:T(8,128)(2,1)} %get-tuple-element.51), channel_id=1, source_target_pairs={{0,20},{4,16},{8,28},{12,24},{16,4},{20,0},{24,12},{28,8},{1,21},{... | collective-permute-start | bytes 860168 | tf_op jit(solution)/shard_map/ppermute | solution.py:628
  25.2 8.6 %collective-permute-done.3.refs_5_ = bf16[1120,128]{1,0:T(8,128)(2,1)S(1)} collective-permute-done((bf16[1120,128]{1,0:T(8,128)(2,1)}, bf16[1120,128]{1,0:T(8,128)(2,1)S(1)}, u32[]{:S(2)}, u32[]{:S(2)}) %collective-permute-start.3) | collective-permute-done | bytes 286752 | tf_op jit(solution)/shard_map/ppermute | solution.py:628
  33.8 0.0 collective-permute-start.4
  33.8 7.5 %collective-permute-done.5.refs_4_ = bf16[1120,128]{1,0:T(8,128)(2,1)S(1)} collective-permute-done((bf16[1120,128]{1,0:T(8,128)(2,1)}, bf16[1120,128]{1,0:T(8,128)(2,1)S(1)}, u32[]{:S(2)}, u32[]{:S(2)}) %collective-permute-start.5) | collective-permute-done | bytes 286752 | tf_op jit(solution)/shard_map/ppermute | solution.py:628
  41.3 0.0 collective-permute-start.6
  41.3 0.0 collective-permute-done.9.refs_3_
  41.3 0.0 copy-start
  41.3 1.0 %copy-done = bf16[3,544,128]{2,1,0:T(8,128)(2,1)S(1)} copy-done((bf16[3,544,128]{2,1,0:T(8,128)(2,1)S(1)}, bf16[3,544,128]{2,1,0:T(8,128)(2,1)}, u32[]{:S(2)}) %copy-start) | copy-done | bytes 417816
  42.3 0.0 copy-start.1
  42.3 1.0 %copy-done.1 = bf16[1120,128]{1,0:T(8,128)(2,1)S(1)} copy-done((bf16[1120,128]{1,0:T(8,128)(2,1)S(1)}, bf16[1120,128]{1,0:T(8,128)(2,1)}, u32[]{:S(2)}) %copy-start.1) | copy-done | bytes 286744
  43.3 9.3 %lag_sums.3 = (f32[13,3,72,128]{3,2,1,0:T(8,128)S(1)}, f32[3,80,128]{2,1,0:T(8,128)S(1)}) custom-call(bf16[3,544,128]{2,1,0:T(8,128)(2,1)S(1)} %copy-done, bf16[1120,128]{1,0:T(8,128)(2,1)S(1)} %copy-done.1, bf16[1040,128]{1,0:T(8,128)(2,1)S(1)} %collective-permute-done.2.refs_2_, bf16[80,128]{1,0:T(8,128)(2,1)S(1)} %collective-permute-done.9.refs_3_, ...), custom_call_target="tpu_custom_call" | custom-call | flops 3000000000 | bytes 10000000 | tf_op jit(solution)/shard_map/lag_sums/pallas_call | solution.py:595
  52.6 0.0 collective-permute-done.7.refs_1_
  52.6 0.0 collective-permute-done.8.refs_2_
  52.6 4.4 %lag_sums.4 = (f32[13,3,72,128]{3,2,1,0:T(8,128)S(1)}, f32[3,80,128]{2,1,0:T(8,128)S(1)}) custom-call(bf16[3,544,128]{2,1,0:T(8,128)(2,1)S(1)} %copy-done, bf16[1120,128]{1,0:T(8,128)(2,1)S(1)} %collective-permute-done.7.refs_1_, bf16[1120,128]{1,0:T(8,128)(2,1)S(1)} %collective-permute-done.8.refs_2_, f32[13,3,72,128]{3,2,1,0:T(8,128)S(1)} %get-tuple-element.57.refs_3_, ...), custom_call_target="tpu_custom_call" | custom-call | flops 1800000000 | bytes 6000000 | tf_op jit(solution)/shard_map/lag_sums/pallas_call | solution.py:595
  57.0 8.9 %collective-permute-done.6.refs_1_ = bf16[1120,128]{1,0:T(8,128)(2,1)S(1)} collective-permute-done((bf16[1120,128]{1,0:T(8,128)(2,1)}, bf16[1120,128]{1,0:T(8,128)(2,1)S(1)}, u32[]{:S(2)}, u32[]{:S(2)}) %collective-permute-start.6) | collective-permute-done | bytes 286752 | tf_op jit(solution)/shard_map/ppermute | solution.py:628
  66.0 3.0 %lag_sums.5 = (f32[13,3,72,128]{3,2,1,0:T(8,128)S(1)}, f32[3,80,128]{2,1,0:T(8,128)S(1)}) custom-call(bf16[3,544,128]{2,1,0:T(8,128)(2,1)S(1)} %copy-done, bf16[1120,128]{1,0:T(8,128)(2,1)S(1)} %collective-permute-done.6.refs_1_, f32[13,3,72,128]{3,2,1,0:T(8,128)S(1)} %get-tuple-element.59.refs_2_, f32[3,80,128]{2,1,0:T(8,128)S(1)} %get-tuple-element.60.refs_3_), custom_call_target="tpu_custom_call" | custom-call | flops 1200000000 | bytes 4000000 | tf_op jit(solution)/shard_map/lag_sums/pallas_call | solution.py:595
  68.9 0.0 collective-permute-done.4.refs_1_
  68.9 5.4 %lag_maps.1 = f32[25,64,256]{2,1,0:T(8,128)} custom-call(bf16[3,544,128]{2,1,0:T(8,128)(2,1)S(1)} %copy-done, bf16[1120,128]{1,0:T(8,128)(2,1)S(1)} %collective-permute-done.4.refs_1_, f32[13,3,72,128]{3,2,1,0:T(8,128)S(1)} %get-tuple-element.61.refs_2_, f32[3,80,128]{2,1,0:T(8,128)S(1)} %get-tuple-element.62.refs_3_), custom_call_target="tpu_custom_call" | custom-call | flops 1200000000 | bytes 4000000 | tf_op jit(solution)/shard_map/lag_maps/pallas_call | solution.py:595
Async XLA Ops:
  3.8 16.4 %collective-permute-start.2 = (bf16[1040,128]{1,0:T(8,128)(2,1)}, bf16[1040,128]{1,0:T(8,128)(2,1)S(1)}, u32[]{:S(2)}, u32[]{:S(2)}) collective-permute-start(bf16[1040,128]{1,0:T(8,128)(2,1)} %pack_one.1), channel_id=1, source_target_pairs={{0,16},{4,20},{8,24},{12,28},{16,0},{20,4},{24,8},{28,12},{1,17},{... | collective-permute-start | bytes 798728 | tf_op jit(solution)/shard_map/ppermute | solution.py:628
  7.2 6.1 %collective-permute-start.1 = (bf16[8,2,2048]{2,1,0:T(2,128)(2,1)S(1)}, bf16[8,2,2048]{2,1,0:T(2,128)(2,1)S(1)}, u32[]{:S(2)}, u32[]{:S(2)}) collective-permute-start(bf16[8,2,2048]{2,1,0:T(2,128)(2,1)S(1)} %get-tuple-element.63), channel_id=1, source_target_pairs={{1,0},{2,1},{3,2},{5,4},{6,5},{7,6},{9,8},{10,9},{11,10},{13,12},{... | collective-permute-start | bytes 196616 | tf_op jit(solution)/shard_map/ppermute | solution.py:634
  10.1 4.4 %collective-permute-start = (bf16[8,2,2048]{2,1,0:T(2,128)(2,1)S(1)}, bf16[8,2,2048]{2,1,0:T(2,128)(2,1)S(1)}, u32[]{:S(2)}, u32[]{:S(2)}) collective-permute-start(bf16[8,2,2048]{2,1,0:T(2,128)(2,1)S(1)} %get-tuple-element.64), channel_id=1, source_target_pairs={{0,1},{1,2},{2,3},{4,5},{5,6},{6,7},{8,9},{9,10},{10,11},{12,13},{... | collective-permute-start | bytes 196616 | tf_op jit(solution)/shard_map/ppermute | solution.py:633
  13.4 1.1 %copy-start.2 = (bf16[8,2,2048]{2,1,0:T(2,128)(2,1)}, bf16[8,2,2048]{2,1,0:T(2,128)(2,1)S(1)}, u32[]{:S(2)}) copy-start(bf16[8,2,2048]{2,1,0:T(2,128)(2,1)S(1)} %collective-permute-done.1.refs_3_) | copy-start | bytes 196612
  14.5 0.6 copy-start.3
  20.2 13.6 %collective-permute-start.3 = (bf16[1120,128]{1,0:T(8,128)(2,1)}, bf16[1120,128]{1,0:T(8,128)(2,1)S(1)}, u32[]{:S(2)}, u32[]{:S(2)}) collective-permute-start(bf16[1120,128]{1,0:T(8,128)(2,1)} %get-tuple-element.43), channel_id=1, source_target_pairs={{0,8},{4,12},{8,0},{12,4},{16,24},{20,28},{24,16},{28,20},{1,9},{5... | collective-permute-start | bytes 860168 | tf_op jit(solution)/shard_map/ppermute | solution.py:628
  20.4 20.9 %collective-permute-start.5 = (bf16[1120,128]{1,0:T(8,128)(2,1)}, bf16[1120,128]{1,0:T(8,128)(2,1)S(1)}, u32[]{:S(2)}, u32[]{:S(2)}) collective-permute-start(bf16[1120,128]{1,0:T(8,128)(2,1)} %get-tuple-element.46), channel_id=1, source_target_pairs={{0,4},{4,0},{8,12},{12,8},{16,20},{20,16},{24,28},{28,24},{1,5},{5... | collective-permute-start | bytes 860168 | tf_op jit(solution)/shard_map/ppermute | solution.py:628
  20.7 20.7 %collective-permute-start.9 = (bf16[80,128]{1,0:T(8,128)(2,1)}, bf16[80,128]{1,0:T(8,128)(2,1)S(1)}, u32[]{:S(2)}, u32[]{:S(2)}) collective-permute-start(bf16[80,128]{1,0:T(8,128)(2,1)} %get-tuple-element.54), channel_id=1, source_target_pairs={{0,16},{4,20},{8,24},{12,28},{16,0},{20,4},{24,8},{28,12},{1,17},{... | collective-permute-start | bytes 61448 | tf_op jit(solution)/shard_map/ppermute | solution.py:637
  21.4 31.2 %collective-permute-start.7 = (bf16[1120,128]{1,0:T(8,128)(2,1)}, bf16[1120,128]{1,0:T(8,128)(2,1)S(1)}, u32[]{:S(2)}, u32[]{:S(2)}) collective-permute-start(bf16[1120,128]{1,0:T(8,128)(2,1)} %get-tuple-element.50), channel_id=1, source_target_pairs={{0,12},{4,8},{8,4},{12,0},{16,28},{20,24},{24,20},{28,16},{1,13},{... | collective-permute-start | bytes 860168 | tf_op jit(solution)/shard_map/ppermute | solution.py:628
  23.8 28.9 %collective-permute-start.8 = (bf16[1120,128]{1,0:T(8,128)(2,1)}, bf16[1120,128]{1,0:T(8,128)(2,1)S(1)}, u32[]{:S(2)}, u32[]{:S(2)}) collective-permute-start(bf16[1120,128]{1,0:T(8,128)(2,1)} %get-tuple-element.51), channel_id=1, source_target_pairs={{0,20},{4,16},{8,28},{12,24},{16,4},{20,0},{24,12},{28,8},{1,21},{... | collective-permute-start | bytes 860168 | tf_op jit(solution)/shard_map/ppermute | solution.py:628
  33.8 35.1 %collective-permute-start.4 = (bf16[1120,128]{1,0:T(8,128)(2,1)}, bf16[1120,128]{1,0:T(8,128)(2,1)S(1)}, u32[]{:S(2)}, u32[]{:S(2)}) collective-permute-start(bf16[1120,128]{1,0:T(8,128)(2,1)} %get-tuple-element.44), channel_id=1, source_target_pairs={{0,28},{4,24},{8,20},{12,16},{16,12},{20,8},{24,4},{28,0},{1,29},{... | collective-permute-start | bytes 860168 | tf_op jit(solution)/shard_map/ppermute | solution.py:628
  41.3 24.6 %collective-permute-start.6 = (bf16[1120,128]{1,0:T(8,128)(2,1)}, bf16[1120,128]{1,0:T(8,128)(2,1)S(1)}, u32[]{:S(2)}, u32[]{:S(2)}) collective-permute-start(bf16[1120,128]{1,0:T(8,128)(2,1)} %get-tuple-element.47), channel_id=1, source_target_pairs={{0,24},{4,28},{8,16},{12,20},{16,8},{20,12},{24,0},{28,4},{1,25},{... | collective-permute-start | bytes 860168 | tf_op jit(solution)/shard_map/ppermute | solution.py:628
  41.3 1.0 %copy-start = (bf16[3,544,128]{2,1,0:T(8,128)(2,1)S(1)}, bf16[3,544,128]{2,1,0:T(8,128)(2,1)}, u32[]{:S(2)}) copy-start(bf16[3,544,128]{2,1,0:T(8,128)(2,1)} %get-tuple-element.34.refs_0_) | copy-start | bytes 1253380
  42.3 1.0 %copy-start.1 = (bf16[1120,128]{1,0:T(8,128)(2,1)S(1)}, bf16[1120,128]{1,0:T(8,128)(2,1)}, u32[]{:S(2)}) copy-start(bf16[1120,128]{1,0:T(8,128)(2,1)} %get-tuple-element.52.refs_1_) | copy-start | bytes 860164

commit v3 on v2

--- a/solution.py
+++ b/solution.py
@@ -638,7 +638,7 @@
     for k in far[1:2] + near:
         send(k, packed[k], far[0])
     for n, k in enumerate(far[2:]):
-        send(k, packed[k], near[n % len(near)])
+        send(k, packed[k], far[1] if n == 0 else near[0])
 
     def sums(group, prior=None, last=False):
         blocks = [(moved[k], around) if k == far[0] else (moved[k],) for k in group]
@@ -646,8 +646,7 @@
 
     moved[0] = packed[0]
     prior = sums([0] + far[:1] + near[:-1])
-    prior = sums(near[-1:] + far[1:-2], prior)
-    prior = sums(far[-2:-1], prior)
+    prior = sums(near[-1:] + far[1:-1], prior)
     return sums(far[-1:], prior, True)
 
 

time: 74.9 us -> 70 us (0.935)
  the two profiles are of different devices: /device:TPU:11 before, /device:TPU:25 now
where the time goes in v3:
time: 70 us; the launch traced here: 69.7 us
  Pallas kernels  30.9 us (44%)
  waiting for transfers between devices  18.3 us (26%)
  starting transfers between devices  16.1 us (23%)
  local copies, waits for them, and re-layouts  3.71 us (5%)
    pallas_call x3, Pallas kernels, lag_sums(): pl.pallas_call(lambda *refs: lag_kernel(tiles, rows, frames, counts, prio...  22.6 us
    ppermute x7, waiting for transfers between devices, send(): lax.ppermute(payload, 'frame', [(i, i ^ k) for i in range(peers)])  17 us
    ppermute x7, starting transfers between devices, send(): lax.ppermute(payload, 'frame', [(i, i ^ k) for i in range(peers)])  9.51 us
    pallas_call x1, Pallas kernels, pack_rest(): pl.pallas_call(lambda *refs: pack_kernel(tiles, skip, *refs), out_shape=[...  5.14 us
    pallas_call x1, Pallas kernels, pack_one(): pl.pallas_call(lambda *refs: pack_one_kernel(tiles, *refs), out_shape=jax...  3.2 us
    ppermute x1, starting transfers between devices, body(): above = lax.ppermute(last, 'strip', up)  3.05 us
    ppermute x1, starting transfers between devices, body(): below = lax.ppermute(initial, 'strip', down)  2.86 us
    unnamed x10, local copies, waits for them, and re-layouts  2.58 us
  transfers between devices with their start and end apart: 10, of which 4 were waited for; matrix products, arithmetic and copies ran while one was open for 2% of the time, Pallas kernels for 32%

profile of v3, /device:TPU:25, one launch (start us, length us, event | category | flops | bytes accessed | tf_op | source)
XLA Modules:
  0.0 69.7 jit_solution(5316578190471709738)
XLA Ops:
  0.0 0.6 pad_add_fusion.refs_0_
  0.6 3.2 %pack_one.1 = bf16[1040,128]{1,0:T(8,128)(2,1)} custom-call(s32[2]{0:T(128)} %pad_add_fusion.refs_0_, bf16[8,64,2048]{2,1,0:T(8,128)(2,1)} %refs_3_.1, bf16[8,64,2048]{2,1,0:T(8,128)(2,1)} %refs_3_.1, bf16[8,64,2048]{2,1,0:T(8,128)(2,1)} %refs_3_.1), custom_call_target="tpu_custom_call" | custom-call | flops 900000000 | bytes 3000000 | tf_op jit(solution)/shard_map/pack_one/pallas_call | solution.py:138
  3.8 0.1 collective-permute-start.2
  3.8 1.1 %fusion = (bf16[8,2,2048]{2,1,0:T(2,128)(2,1)S(1)}, bf16[8,2,2048]{2,1,0:T(2,128)(2,1)S(1)}) fusion(bf16[8,64,2048]{2,1,0:T(8,128)(2,1)} %refs_3_.1), kind=kLoop, calls=%fused_computation.1 | loop fusion | bytes 262144 | tf_op jit(solution)/shard_map/slice | solution.py:632
  5.0 2.9 %collective-permute-start.1 = (bf16[8,2,2048]{2,1,0:T(2,128)(2,1)S(1)}, bf16[8,2,2048]{2,1,0:T(2,128)(2,1)S(1)}, u32[]{:S(2)}, u32[]{:S(2)}) collective-permute-start(bf16[8,2,2048]{2,1,0:T(2,128)(2,1)S(1)} %get-tuple-element.59), channel_id=1, source_target_pairs={{1,0},{2,1},{3,2},{5,4},{6,5},{7,6},{9,8},{10,9},{11,10},{13,12},{... | collective-permute-start | bytes 196616 | tf_op jit(solution)/shard_map/ppermute | solution.py:634
  7.8 3.0 %collective-permute-start = (bf16[8,2,2048]{2,1,0:T(2,128)(2,1)S(1)}, bf16[8,2,2048]{2,1,0:T(2,128)(2,1)S(1)}, u32[]{:S(2)}, u32[]{:S(2)}) collective-permute-start(bf16[8,2,2048]{2,1,0:T(2,128)(2,1)S(1)} %get-tuple-element.60), channel_id=1, source_target_pairs={{0,1},{1,2},{2,3},{4,5},{5,6},{6,7},{8,9},{9,10},{10,11},{12,13},{... | collective-permute-start | bytes 196616 | tf_op jit(solution)/shard_map/ppermute | solution.py:633
  10.9 0.0 collective-permute-done.1.refs_3_
  10.9 0.0 copy-start.3
  10.9 1.3 %collective-permute-done.refs_2_ = bf16[8,2,2048]{2,1,0:T(2,128)(2,1)S(1)} collective-permute-done((bf16[8,2,2048]{2,1,0:T(2,128)(2,1)S(1)}, bf16[8,2,2048]{2,1,0:T(2,128)(2,1)S(1)}, u32[]{:S(2)}, u32[]{:S(2)}) %collective-permute-start) | collective-permute-done | bytes 65568 | tf_op jit(solution)/shard_map/ppermute | solution.py:633
  12.2 0.0 copy-start.4
  12.2 0.0 copy-done.3
  12.2 0.6 copy-done.4
  12.8 5.1 %pack_rest.1 = (bf16[1120,128]{1,0:T(8,128)(2,1)}, bf16[1120,128]{1,0:T(8,128)(2,1)}, bf16[1120,128]{1,0:T(8,128)(2,1)}, bf16[1120,128]{1,0:T(8,128)(2,1)}, bf16...) custom-call(s32[1]{0:T(128)} %bitcast.refs_0_, ...), custom_call_target="tpu_custom_call" | custom-call | flops 1500000000 | bytes 5000000 | tf_op jit(solution)/shard_map/pack_rest/pallas_call | solution.py:233
  18.0 0.9 %collective-permute-done.2.refs_2_ = bf16[1040,128]{1,0:T(8,128)(2,1)S(1)} collective-permute-done((bf16[1040,128]{1,0:T(8,128)(2,1)}, bf16[1040,128]{1,0:T(8,128)(2,1)S(1)}, u32[]{:S(2)}, u32[]{:S(2)}) %collective-permute-start.2) | collective-permute-done | bytes 266272 | tf_op jit(solution)/shard_map/ppermute | solution.py:628
  18.8 2.4 %collective-permute-start.6 = (bf16[1120,128]{1,0:T(8,128)(2,1)}, bf16[1120,128]{1,0:T(8,128)(2,1)S(1)}, u32[]{:S(2)}, u32[]{:S(2)}) collective-permute-start(bf16[1120,128]{1,0:T(8,128)(2,1)} %get-tuple-element.47), channel_id=1, source_target_pairs={{0,20},{4,16},{8,28},{12,24},{16,4},{20,0},{24,12},{28,8},{1,21},{... | collective-permute-start | bytes 860168 | tf_op jit(solution)/shard_map/ppermute | solution.py:628
  21.2 0.3 collective-permute-start.3
  21.5 0.2 collective-permute-start.9
  21.6 0.7 %collective-permute-start.8 = (bf16[80,128]{1,0:T(8,128)(2,1)}, bf16[80,128]{1,0:T(8,128)(2,1)S(1)}, u32[]{:S(2)}, u32[]{:S(2)}) collective-permute-start(bf16[80,128]{1,0:T(8,128)(2,1)} %get-tuple-element.52), channel_id=1, source_target_pairs={{0,16},{4,20},{8,24},{12,28},{16,0},{20,4},{24,8},{28,12},{1,17},{... | collective-permute-start | bytes 61448 | tf_op jit(solution)/shard_map/ppermute | solution.py:637
  22.4 2.4 %collective-permute-start.5 = (bf16[1120,128]{1,0:T(8,128)(2,1)}, bf16[1120,128]{1,0:T(8,128)(2,1)S(1)}, u32[]{:S(2)}, u32[]{:S(2)}) collective-permute-start(bf16[1120,128]{1,0:T(8,128)(2,1)} %get-tuple-element.45), channel_id=1, source_target_pairs={{0,12},{4,8},{8,4},{12,0},{16,28},{20,24},{24,20},{28,16},{1,13},{... | collective-permute-start | bytes 860168 | tf_op jit(solution)/shard_map/ppermute | solution.py:628
  24.7 9.6 %collective-permute-done.6.refs_2_ = bf16[1120,128]{1,0:T(8,128)(2,1)S(1)} collective-permute-done((bf16[1120,128]{1,0:T(8,128)(2,1)}, bf16[1120,128]{1,0:T(8,128)(2,1)S(1)}, u32[]{:S(2)}, u32[]{:S(2)}) %collective-permute-start.6) | collective-permute-done | bytes 286752 | tf_op jit(solution)/shard_map/ppermute | solution.py:628
  34.4 2.4 %collective-permute-start.7 = (bf16[1120,128]{1,0:T(8,128)(2,1)}, bf16[1120,128]{1,0:T(8,128)(2,1)S(1)}, u32[]{:S(2)}, u32[]{:S(2)}) collective-permute-start(bf16[1120,128]{1,0:T(8,128)(2,1)} %get-tuple-element.49), channel_id=1, source_target_pairs={{0,24},{4,28},{8,16},{12,20},{16,8},{20,12},{24,0},{28,4},{1,25},{... | collective-permute-start | bytes 860168 | tf_op jit(solution)/shard_map/ppermute | solution.py:628
  36.8 0.0 collective-permute-done.3.refs_4_
  36.8 1.8 %collective-permute-start.4 = (bf16[1120,128]{1,0:T(8,128)(2,1)}, bf16[1120,128]{1,0:T(8,128)(2,1)S(1)}, u32[]{:S(2)}, u32[]{:S(2)}) collective-permute-start(bf16[1120,128]{1,0:T(8,128)(2,1)} %get-tuple-element.40), channel_id=1, source_target_pairs={{0,28},{4,24},{8,20},{12,16},{16,12},{20,8},{24,4},{28,0},{1,29},{... | collective-permute-start | bytes 860168 | tf_op jit(solution)/shard_map/ppermute | solution.py:628
  38.6 0.0 collective-permute-done.8.refs_3_
  38.6 0.0 collective-permute-done.9.refs_5_
  38.6 0.0 copy-start
  38.6 1.0 %copy-done = bf16[3,544,128]{2,1,0:T(8,128)(2,1)S(1)} copy-done((bf16[3,544,128]{2,1,0:T(8,128)(2,1)S(1)}, bf16[3,544,128]{2,1,0:T(8,128)(2,1)}, u32[]{:S(2)}) %copy-start) | copy-done | bytes 417816
  39.6 0.0 copy-start.2
  39.6 1.0 %copy-done.2 = bf16[1120,128]{1,0:T(8,128)(2,1)S(1)} copy-done((bf16[1120,128]{1,0:T(8,128)(2,1)S(1)}, bf16[1120,128]{1,0:T(8,128)(2,1)}, u32[]{:S(2)}) %copy-start.2) | copy-done | bytes 286744
  40.6 0.0 copy-start.1
  40.6 9.2 %lag_sums.2 = (f32[13,3,72,128]{3,2,1,0:T(8,128)S(1)}, f32[3,80,128]{2,1,0:T(8,128)S(1)}) custom-call(bf16[3,544,128]{2,1,0:T(8,128)(2,1)S(1)} %copy-done, bf16[1120,128]{1,0:T(8,128)(2,1)S(1)} %copy-done.2, bf16[1040,128]{1,0:T(8,128)(2,1)S(1)} %collective-permute-done.2.refs_2_, bf16[80,128]{1,0:T(8,128)(2,1)S(1)} %collective-permute-done.8.refs_3_, ...), custom_call_target="tpu_custom_call" | custom-call | flops 3000000000 | bytes 10000000 | tf_op jit(solution)/shard_map/lag_sums/pallas_call | solution.py:595
  49.8 6.5 %collective-permute-done.5.refs_1_ = bf16[1120,128]{1,0:T(8,128)(2,1)S(1)} collective-permute-done((bf16[1120,128]{1,0:T(8,128)(2,1)}, bf16[1120,128]{1,0:T(8,128)(2,1)S(1)}, u32[]{:S(2)}, u32[]{:S(2)}) %collective-permute-start.5) | collective-permute-done | bytes 286752 | tf_op jit(solution)/shard_map/ppermute | solution.py:628
  56.3 0.0 collective-permute-done.7.refs_3_
  56.3 0.0 copy-done.1
  56.3 8.0 %lag_sums.3 = (f32[13,3,72,128]{3,2,1,0:T(8,128)S(1)}, f32[3,80,128]{2,1,0:T(8,128)S(1)}) custom-call(bf16[3,544,128]{2,1,0:T(8,128)(2,1)S(1)} %copy-done.1, bf16[1120,128]{1,0:T(8,128)(2,1)S(1)} %collective-permute-done.5.refs_1_, bf16[1120,128]{1,0:T(8,128)(2,1)S(1)} %collective-permute-done.6.refs_2_, ...), custom_call_target="tpu_custom_call" | custom-call | flops 2400000000 | bytes 8000000 | tf_op jit(solution)/shard_map/lag_sums/pallas_call | solution.py:595
  64.3 0.0 collective-permute-done.4.refs_1_
  64.3 5.4 %lag_maps.1 = f32[25,64,256]{2,1,0:T(8,128)} custom-call(bf16[3,544,128]{2,1,0:T(8,128)(2,1)S(1)} %copy-done.1, bf16[1120,128]{1,0:T(8,128)(2,1)S(1)} %collective-permute-done.4.refs_1_, f32[13,3,72,128]{3,2,1,0:T(8,128)S(1)} %get-tuple-element.57.refs_2_, f32[3,80,128]{2,1,0:T(8,128)S(1)} %get-tuple-element.58.refs_3_), custom_call_target="tpu_custom_call" | custom-call | flops 1200000000 | bytes 4000000 | tf_op jit(solution)/shard_map/lag_maps/pallas_call | solution.py:595
Async XLA Ops:
  3.8 15.0 %collective-permute-start.2 = (bf16[1040,128]{1,0:T(8,128)(2,1)}, bf16[1040,128]{1,0:T(8,128)(2,1)S(1)}, u32[]{:S(2)}, u32[]{:S(2)}) collective-permute-start(bf16[1040,128]{1,0:T(8,128)(2,1)} %pack_one.1), channel_id=1, source_target_pairs={{0,16},{4,20},{8,24},{12,28},{16,0},{20,4},{24,8},{28,12},{1,17},{... | collective-permute-start | bytes 798728 | tf_op jit(solution)/shard_map/ppermute | solution.py:628
  5.0 5.9 %collective-permute-start.1 = (bf16[8,2,2048]{2,1,0:T(2,128)(2,1)S(1)}, bf16[8,2,2048]{2,1,0:T(2,128)(2,1)S(1)}, u32[]{:S(2)}, u32[]{:S(2)}) collective-permute-start(bf16[8,2,2048]{2,1,0:T(2,128)(2,1)S(1)} %get-tuple-element.59), channel_id=1, source_target_pairs={{1,0},{2,1},{3,2},{5,4},{6,5},{7,6},{9,8},{10,9},{11,10},{13,12},{... | collective-permute-start | bytes 196616 | tf_op jit(solution)/shard_map/ppermute | solution.py:634
  7.8 4.4 %collective-permute-start = (bf16[8,2,2048]{2,1,0:T(2,128)(2,1)S(1)}, bf16[8,2,2048]{2,1,0:T(2,128)(2,1)S(1)}, u32[]{:S(2)}, u32[]{:S(2)}) collective-permute-start(bf16[8,2,2048]{2,1,0:T(2,128)(2,1)S(1)} %get-tuple-element.60), channel_id=1, source_target_pairs={{0,1},{1,2},{2,3},{4,5},{5,6},{6,7},{8,9},{9,10},{10,11},{12,13},{... | collective-permute-start | bytes 196616 | tf_op jit(solution)/shard_map/ppermute | solution.py:633
  10.9 1.3 %copy-start.3 = (bf16[8,2,2048]{2,1,0:T(2,128)(2,1)}, bf16[8,2,2048]{2,1,0:T(2,128)(2,1)S(1)}, u32[]{:S(2)}) copy-start(bf16[8,2,2048]{2,1,0:T(2,128)(2,1)S(1)} %collective-permute-done.1.refs_3_) | copy-start | bytes 196612
  12.2 0.6 copy-start.4
  18.8 15.6 %collective-permute-start.6 = (bf16[1120,128]{1,0:T(8,128)(2,1)}, bf16[1120,128]{1,0:T(8,128)(2,1)S(1)}, u32[]{:S(2)}, u32[]{:S(2)}) collective-permute-start(bf16[1120,128]{1,0:T(8,128)(2,1)} %get-tuple-element.47), channel_id=1, source_target_pairs={{0,20},{4,16},{8,28},{12,24},{16,4},{20,0},{24,12},{28,8},{1,21},{... | collective-permute-start | bytes 860168 | tf_op jit(solution)/shard_map/ppermute | solution.py:628
  21.2 15.6 %collective-permute-start.3 = (bf16[1120,128]{1,0:T(8,128)(2,1)}, bf16[1120,128]{1,0:T(8,128)(2,1)S(1)}, u32[]{:S(2)}, u32[]{:S(2)}) collective-permute-start(bf16[1120,128]{1,0:T(8,128)(2,1)} %get-tuple-element.39), channel_id=1, source_target_pairs={{0,4},{4,0},{8,12},{12,8},{16,20},{20,16},{24,28},{28,24},{1,5},{5... | collective-permute-start | bytes 860168 | tf_op jit(solution)/shard_map/ppermute | solution.py:628
  21.5 17.2 %collective-permute-start.9 = (bf16[1120,128]{1,0:T(8,128)(2,1)}, bf16[1120,128]{1,0:T(8,128)(2,1)S(1)}, u32[]{:S(2)}, u32[]{:S(2)}) collective-permute-start(bf16[1120,128]{1,0:T(8,128)(2,1)} %get-tuple-element.54), channel_id=1, source_target_pairs={{0,8},{4,12},{8,0},{12,4},{16,24},{20,28},{24,16},{28,20},{1,9},{5... | collective-permute-start | bytes 860168 | tf_op jit(solution)/shard_map/ppermute | solution.py:628
  21.6 17.0 %collective-permute-start.8 = (bf16[80,128]{1,0:T(8,128)(2,1)}, bf16[80,128]{1,0:T(8,128)(2,1)S(1)}, u32[]{:S(2)}, u32[]{:S(2)}) collective-permute-start(bf16[80,128]{1,0:T(8,128)(2,1)} %get-tuple-element.52), channel_id=1, source_target_pairs={{0,16},{4,20},{8,24},{12,28},{16,0},{20,4},{24,8},{28,12},{1,17},{... | collective-permute-start | bytes 61448 | tf_op jit(solution)/shard_map/ppermute | solution.py:637
  22.4 33.9 %collective-permute-start.5 = (bf16[1120,128]{1,0:T(8,128)(2,1)}, bf16[1120,128]{1,0:T(8,128)(2,1)S(1)}, u32[]{:S(2)}, u32[]{:S(2)}) collective-permute-start(bf16[1120,128]{1,0:T(8,128)(2,1)} %get-tuple-element.45), channel_id=1, source_target_pairs={{0,12},{4,8},{8,4},{12,0},{16,28},{20,24},{24,20},{28,16},{1,13},{... | collective-permute-start | bytes 860168 | tf_op jit(solution)/shard_map/ppermute | solution.py:628
  34.4 21.9 %collective-permute-start.7 = (bf16[1120,128]{1,0:T(8,128)(2,1)}, bf16[1120,128]{1,0:T(8,128)(2,1)S(1)}, u32[]{:S(2)}, u32[]{:S(2)}) collective-permute-start(bf16[1120,128]{1,0:T(8,128)(2,1)} %get-tuple-element.49), channel_id=1, source_target_pairs={{0,24},{4,28},{8,16},{12,20},{16,8},{20,12},{24,0},{28,4},{1,25},{... | collective-permute-start | bytes 860168 | tf_op jit(solution)/shard_map/ppermute | solution.py:628
  36.8 27.5 %collective-permute-start.4 = (bf16[1120,128]{1,0:T(8,128)(2,1)}, bf16[1120,128]{1,0:T(8,128)(2,1)S(1)}, u32[]{:S(2)}, u32[]{:S(2)}) collective-permute-start(bf16[1120,128]{1,0:T(8,128)(2,1)} %get-tuple-element.40), channel_id=1, source_target_pairs={{0,28},{4,24},{8,20},{12,16},{16,12},{20,8},{24,4},{28,0},{1,29},{... | collective-permute-start | bytes 860168 | tf_op jit(solution)/shard_map/ppermute | solution.py:628
  38.6 1.0 %copy-start = (bf16[3,544,128]{2,1,0:T(8,128)(2,1)S(1)}, bf16[3,544,128]{2,1,0:T(8,128)(2,1)}, u32[]{:S(2)}) copy-start(bf16[3,544,128]{2,1,0:T(8,128)(2,1)} %get-tuple-element.32.refs_0_) | copy-start | bytes 1253380
  39.6 1.0 %copy-start.2 = (bf16[1120,128]{1,0:T(8,128)(2,1)S(1)}, bf16[1120,128]{1,0:T(8,128)(2,1)}, u32[]{:S(2)}) copy-start(bf16[1120,128]{1,0:T(8,128)(2,1)} %get-tuple-element.50.refs_1_) | copy-start | bytes 860164
  40.6 15.7 %copy-start.1 = (bf16[3,544,128]{2,1,0:T(8,128)(2,1)S(1)}, bf16[3,544,128]{2,1,0:T(8,128)(2,1)}, u32[]{:S(2)}) copy-start(bf16[3,544,128]{2,1,0:T(8,128)(2,1)} %get-tuple-element.32.refs_0_) | copy-start | bytes 1253380

commit v4 on v3

--- a/solution.py
+++ b/solution.py
@@ -645,8 +645,9 @@
         return lag_sums(pivot, blocks, rows, tiles, frames, prior, last)
 
     moved[0] = packed[0]
-    prior = sums([0] + far[:1] + near[:-1])
-    prior = sums(near[-1:] + far[1:-1], prior)
+    prior = sums([0])
+    prior = sums(far[:2] + near[:-1], prior)
+    prior = sums(near[-1:] + far[2:-1], prior)
     return sums(far[-1:], prior, True)
 
 

time: 70 us -> 67.5 us (0.964)
  the two profiles are of different devices: /device:TPU:25 before, /device:TPU:11 now
where the time goes in v4:
time: 67.5 us; the launch traced here: 67.2 us
  Pallas kernels  30.6 us (45%)
  waiting for transfers between devices  17 us (25%)
  starting transfers between devices  15.2 us (23%)
  local copies, waits for them, and re-layouts  3.72 us (6%)
    pallas_call x4, Pallas kernels, lag_sums(): pl.pallas_call(lambda *refs: lag_kernel(tiles, rows, frames, counts, prio...  22.2 us
    ppermute x7, waiting for transfers between devices, send(): lax.ppermute(payload, 'frame', [(i, i ^ k) for i in range(peers)])  15.7 us
    ppermute x7, starting transfers between devices, send(): lax.ppermute(payload, 'frame', [(i, i ^ k) for i in range(peers)])  7.6 us
    pallas_call x1, Pallas kernels, pack_rest(): pl.pallas_call(lambda *refs: pack_kernel(tiles, skip, *refs), out_shape=[...  5.14 us
    pallas_call x1, Pallas kernels, pack_one(): pl.pallas_call(lambda *refs: pack_one_kernel(tiles, *refs), out_shape=jax...  3.21 us
    ppermute x1, starting transfers between devices, body(): above = lax.ppermute(last, 'strip', up)  3.05 us
    ppermute x1, starting transfers between devices, body(): below = lax.ppermute(initial, 'strip', down)  2.86 us
    unnamed x12, local copies, waits for them, and re-layouts  2.58 us
  transfers between devices with their start and end apart: 10, of which 6 were waited for; matrix products, arithmetic and copies ran while one was open for 2% of the time, Pallas kernels for 33%

profile of v4, /device:TPU:11, one launch (start us, length us, event | category | flops | bytes accessed | tf_op | source)
XLA Modules:
  0.0 67.2 jit_solution(10598558985899889287)
XLA Ops:
  0.0 0.7 pad_add_fusion.refs_0_
  0.7 3.2 %pack_one.1 = bf16[1040,128]{1,0:T(8,128)(2,1)} custom-call(s32[2]{0:T(128)} %pad_add_fusion.refs_0_, bf16[8,64,2048]{2,1,0:T(8,128)(2,1)} %refs_3_.1, bf16[8,64,2048]{2,1,0:T(8,128)(2,1)} %refs_3_.1, bf16[8,64,2048]{2,1,0:T(8,128)(2,1)} %refs_3_.1), custom_call_target="tpu_custom_call" | custom-call | flops 900000000 | bytes 3000000 | tf_op jit(solution)/shard_map/pack_one/pallas_call | solution.py:138
  3.9 2.3 %collective-permute-start.2 = (bf16[1040,128]{1,0:T(8,128)(2,1)}, bf16[1040,128]{1,0:T(8,128)(2,1)S(1)}, u32[]{:S(2)}, u32[]{:S(2)}) collective-permute-start(bf16[1040,128]{1,0:T(8,128)(2,1)} %pack_one.1), channel_id=1, source_target_pairs={{0,16},{4,20},{8,24},{12,28},{16,0},{20,4},{24,8},{28,12},{1,17},{... | collective-permute-start | bytes 798728 | tf_op jit(solution)/shard_map/ppermute | solution.py:628
  6.2 1.1 %fusion = (bf16[8,2,2048]{2,1,0:T(2,128)(2,1)S(1)}, bf16[8,2,2048]{2,1,0:T(2,128)(2,1)S(1)}) fusion(bf16[8,64,2048]{2,1,0:T(8,128)(2,1)} %refs_3_.1), kind=kLoop, calls=%fused_computation.1 | loop fusion | bytes 262144 | tf_op jit(solution)/shard_map/slice | solution.py:632
  7.3 2.9 %collective-permute-start.1 = (bf16[8,2,2048]{2,1,0:T(2,128)(2,1)S(1)}, bf16[8,2,2048]{2,1,0:T(2,128)(2,1)S(1)}, u32[]{:S(2)}, u32[]{:S(2)}) collective-permute-start(bf16[8,2,2048]{2,1,0:T(2,128)(2,1)S(1)} %get-tuple-element.63), channel_id=1, source_target_pairs={{1,0},{2,1},{3,2},{5,4},{6,5},{7,6},{9,8},{10,9},{11,10},{13,12},{... | collective-permute-start | bytes 196616 | tf_op jit(solution)/shard_map/ppermute | solution.py:634
  10.2 3.0 %collective-permute-start = (bf16[8,2,2048]{2,1,0:T(2,128)(2,1)S(1)}, bf16[8,2,2048]{2,1,0:T(2,128)(2,1)S(1)}, u32[]{:S(2)}, u32[]{:S(2)}) collective-permute-start(bf16[8,2,2048]{2,1,0:T(2,128)(2,1)S(1)} %get-tuple-element.64), channel_id=1, source_target_pairs={{0,1},{1,2},{2,3},{4,5},{5,6},{6,7},{8,9},{9,10},{10,11},{12,13},{... | collective-permute-start | bytes 196616 | tf_op jit(solution)/shard_map/ppermute | solution.py:633
  13.2 0.2 collective-permute-done.1.refs_3_
  13.4 0.0 copy-start.4
  13.4 1.1 %collective-permute-done.refs_2_ = bf16[8,2,2048]{2,1,0:T(2,128)(2,1)S(1)} collective-permute-done((bf16[8,2,2048]{2,1,0:T(2,128)(2,1)S(1)}, bf16[8,2,2048]{2,1,0:T(2,128)(2,1)S(1)}, u32[]{:S(2)}, u32[]{:S(2)}) %collective-permute-start) | collective-permute-done | bytes 65568 | tf_op jit(solution)/shard_map/ppermute | solution.py:633
  14.5 0.0 copy-start.5
  14.5 0.0 copy-done.4
  14.5 0.6 copy-done.5
  15.2 5.1 %pack_rest.1 = (bf16[1120,128]{1,0:T(8,128)(2,1)}, bf16[1120,128]{1,0:T(8,128)(2,1)}, bf16[1120,128]{1,0:T(8,128)(2,1)}, bf16[1120,128]{1,0:T(8,128)(2,1)}, bf16...) custom-call(s32[1]{0:T(128)} %bitcast.refs_0_, ...), custom_call_target="tpu_custom_call" | custom-call | flops 1500000000 | bytes 5000000 | tf_op jit(solution)/shard_map/pack_rest/pallas_call | solution.py:233
  20.3 0.0 collective-permute-done.2.refs_1_
  20.3 0.9 %collective-permute-start.6 = (bf16[1120,128]{1,0:T(8,128)(2,1)}, bf16[1120,128]{1,0:T(8,128)(2,1)S(1)}, u32[]{:S(2)}, u32[]{:S(2)}) collective-permute-start(bf16[1120,128]{1,0:T(8,128)(2,1)} %get-tuple-element.49), channel_id=1, source_target_pairs={{0,20},{4,16},{8,28},{12,24},{16,4},{20,0},{24,12},{28,8},{1,21},{... | collective-permute-start | bytes 860168 | tf_op jit(solution)/shard_map/ppermute | solution.py:628
  21.2 1.2 %collective-permute-start.3 = (bf16[1120,128]{1,0:T(8,128)(2,1)}, bf16[1120,128]{1,0:T(8,128)(2,1)S(1)}, u32[]{:S(2)}, u32[]{:S(2)}) collective-permute-start(bf16[1120,128]{1,0:T(8,128)(2,1)} %get-tuple-element.41), channel_id=1, source_target_pairs={{0,4},{4,0},{8,12},{12,8},{16,20},{20,16},{24,28},{28,24},{1,5},{5... | collective-permute-start | bytes 860168 | tf_op jit(solution)/shard_map/ppermute | solution.py:628
  22.4 0.0 collective-permute-start.9
  22.4 1.6 %collective-permute-start.8 = (bf16[80,128]{1,0:T(8,128)(2,1)}, bf16[80,128]{1,0:T(8,128)(2,1)S(1)}, u32[]{:S(2)}, u32[]{:S(2)}) collective-permute-start(bf16[80,128]{1,0:T(8,128)(2,1)} %get-tuple-element.52), channel_id=1, source_target_pairs={{0,16},{4,20},{8,24},{12,28},{16,0},{20,4},{24,8},{28,12},{1,17},{... | collective-permute-start | bytes 61448 | tf_op jit(solution)/shard_map/ppermute | solution.py:637
  24.0 1.3 %collective-permute-start.5 = (bf16[1120,128]{1,0:T(8,128)(2,1)}, bf16[1120,128]{1,0:T(8,128)(2,1)S(1)}, u32[]{:S(2)}, u32[]{:S(2)}) collective-permute-start(bf16[1120,128]{1,0:T(8,128)(2,1)} %get-tuple-element.47), channel_id=1, source_target_pairs={{0,12},{4,8},{8,4},{12,0},{16,28},{20,24},{24,20},{28,16},{1,13},{... | collective-permute-start | bytes 860168 | tf_op jit(solution)/shard_map/ppermute | solution.py:628
  25.3 7.4 %collective-permute-done.6.refs_3_ = bf16[1120,128]{1,0:T(8,128)(2,1)S(1)} collective-permute-done((bf16[1120,128]{1,0:T(8,128)(2,1)}, bf16[1120,128]{1,0:T(8,128)(2,1)S(1)}, u32[]{:S(2)}, u32[]{:S(2)}) %collective-permute-start.6) | collective-permute-done | bytes 286752 | tf_op jit(solution)/shard_map/ppermute | solution.py:628
  32.6 2.0 %collective-permute-start.7 = (bf16[1120,128]{1,0:T(8,128)(2,1)}, bf16[1120,128]{1,0:T(8,128)(2,1)S(1)}, u32[]{:S(2)}, u32[]{:S(2)}) collective-permute-start(bf16[1120,128]{1,0:T(8,128)(2,1)} %get-tuple-element.50), channel_id=1, source_target_pairs={{0,24},{4,28},{8,16},{12,20},{16,8},{20,12},{24,0},{28,4},{1,25},{... | collective-permute-start | bytes 860168 | tf_op jit(solution)/shard_map/ppermute | solution.py:628
  34.6 0.0 copy-start
  34.6 1.0 %copy-done = bf16[3,544,128]{2,1,0:T(8,128)(2,1)S(1)} copy-done((bf16[3,544,128]{2,1,0:T(8,128)(2,1)S(1)}, bf16[3,544,128]{2,1,0:T(8,128)(2,1)}, u32[]{:S(2)}) %copy-start) | copy-done | bytes 417816
  35.6 0.0 copy-start.2
  35.6 1.0 %copy-done.2 = bf16[1120,128]{1,0:T(8,128)(2,1)S(1)} copy-done((bf16[1120,128]{1,0:T(8,128)(2,1)S(1)}, bf16[1120,128]{1,0:T(8,128)(2,1)}, u32[]{:S(2)}) %copy-start.2) | copy-done | bytes 286744
  36.6 0.0 copy-start.3
  36.6 0.0 copy-start.1
  36.6 2.9 %lag_sums.3 = (f32[13,3,72,128]{3,2,1,0:T(8,128)S(1)}, f32[3,80,128]{2,1,0:T(8,128)S(1)}) custom-call(bf16[3,544,128]{2,1,0:T(8,128)(2,1)S(1)} %copy-done, bf16[1120,128]{1,0:T(8,128)(2,1)S(1)} %copy-done.2), custom_call_target="tpu_custom_call" | custom-call | flops 1200000000 | bytes 4000000 | tf_op jit(solution)/shard_map/lag_sums/pallas_call | solution.py:595
  39.5 2.5 %collective-permute-done.3.refs_4_ = bf16[1120,128]{1,0:T(8,128)(2,1)S(1)} collective-permute-done((bf16[1120,128]{1,0:T(8,128)(2,1)}, bf16[1120,128]{1,0:T(8,128)(2,1)S(1)}, u32[]{:S(2)}, u32[]{:S(2)}) %collective-permute-start.3) | collective-permute-done | bytes 286752 | tf_op jit(solution)/shard_map/ppermute | solution.py:628
  42.0 0.0 copy-done.3
  42.0 0.0 collective-permute-start.4
  42.0 0.0 collective-permute-done.8.refs_2_
  42.0 0.0 collective-permute-done.9.refs_5_
  42.0 0.0 copy-done.1
  42.0 9.6 %lag_sums.4 = (f32[13,3,72,128]{3,2,1,0:T(8,128)S(1)}, f32[3,80,128]{2,1,0:T(8,128)S(1)}) custom-call(bf16[3,544,128]{2,1,0:T(8,128)(2,1)S(1)} %copy-done.1, bf16[1040,128]{1,0:T(8,128)(2,1)S(1)} %collective-permute-done.2.refs_1_, bf16[80,128]{1,0:T(8,128)(2,1)S(1)} %collective-permute-done.8.refs_2_, bf16[1120,128]{1,0:T(8,128)(2,1)S(1)} %collective-permute-done.6.refs_3_, ...), custom_call_target="tpu_custom_call" | custom-call | flops 3000000000 | bytes 10000000 | tf_op jit(solution)/shard_map/lag_sums/pallas_call | solution.py:595
  51.6 0.0 collective-permute-done.5.refs_1_
  51.6 1.9 %collective-permute-done.7.refs_2_ = bf16[1120,128]{1,0:T(8,128)(2,1)S(1)} collective-permute-done((bf16[1120,128]{1,0:T(8,128)(2,1)}, bf16[1120,128]{1,0:T(8,128)(2,1)S(1)}, u32[]{:S(2)}, u32[]{:S(2)}) %collective-permute-start.7) | collective-permute-done | bytes 286752 | tf_op jit(solution)/shard_map/ppermute | solution.py:628
  53.6 4.4 %lag_sums.5 = (f32[13,3,72,128]{3,2,1,0:T(8,128)S(1)}, f32[3,80,128]{2,1,0:T(8,128)S(1)}) custom-call(bf16[3,544,128]{2,1,0:T(8,128)(2,1)S(1)} %copy-done.1, bf16[1120,128]{1,0:T(8,128)(2,1)S(1)} %collective-permute-done.5.refs_1_, bf16[1120,128]{1,0:T(8,128)(2,1)S(1)} %collective-permute-done.7.refs_2_, f32[13,3,72,128]{3,2,1,0:T(8,128)S(1)} %get-tuple-element.59.refs_3_, ...), custom_call_target="tpu_custom_call" | custom-call | flops 1800000000 | bytes 6000000 | tf_op jit(solution)/shard_map/lag_sums/pallas_call | solution.py:595
  58.0 3.9 %collective-permute-done.4.refs_1_ = bf16[1120,128]{1,0:T(8,128)(2,1)S(1)} collective-permute-done((bf16[1120,128]{1,0:T(8,128)(2,1)S(1)}, bf16[1120,128]{1,0:T(8,128)(2,1)S(1)}, u32[]{:S(2)}, u32[]{:S(2)}) %collective-permute-start.4) | collective-permute-done | bytes 286752 | tf_op jit(solution)/shard_map/ppermute | solution.py:628
  61.9 5.4 %lag_maps.1 = f32[25,64,256]{2,1,0:T(8,128)} custom-call(bf16[3,544,128]{2,1,0:T(8,128)(2,1)S(1)} %copy-done.1, bf16[1120,128]{1,0:T(8,128)(2,1)S(1)} %collective-permute-done.4.refs_1_, f32[13,3,72,128]{3,2,1,0:T(8,128)S(1)} %get-tuple-element.61.refs_2_, f32[3,80,128]{2,1,0:T(8,128)S(1)} %get-tuple-element.62.refs_3_), custom_call_target="tpu_custom_call" | custom-call | flops 1200000000 | bytes 4000000 | tf_op jit(solution)/shard_map/lag_maps/pallas_call | solution.py:595
Async XLA Ops:
  3.9 16.4 %collective-permute-start.2 = (bf16[1040,128]{1,0:T(8,128)(2,1)}, bf16[1040,128]{1,0:T(8,128)(2,1)S(1)}, u32[]{:S(2)}, u32[]{:S(2)}) collective-permute-start(bf16[1040,128]{1,0:T(8,128)(2,1)} %pack_one.1), channel_id=1, source_target_pairs={{0,16},{4,20},{8,24},{12,28},{16,0},{20,4},{24,8},{28,12},{1,17},{... | collective-permute-start | bytes 798728 | tf_op jit(solution)/shard_map/ppermute | solution.py:628
  7.3 6.1 %collective-permute-start.1 = (bf16[8,2,2048]{2,1,0:T(2,128)(2,1)S(1)}, bf16[8,2,2048]{2,1,0:T(2,128)(2,1)S(1)}, u32[]{:S(2)}, u32[]{:S(2)}) collective-permute-start(bf16[8,2,2048]{2,1,0:T(2,128)(2,1)S(1)} %get-tuple-element.63), channel_id=1, source_target_pairs={{1,0},{2,1},{3,2},{5,4},{6,5},{7,6},{9,8},{10,9},{11,10},{13,12},{... | collective-permute-start | bytes 196616 | tf_op jit(solution)/shard_map/ppermute | solution.py:634
  10.2 4.4 %collective-permute-start = (bf16[8,2,2048]{2,1,0:T(2,128)(2,1)S(1)}, bf16[8,2,2048]{2,1,0:T(2,128)(2,1)S(1)}, u32[]{:S(2)}, u32[]{:S(2)}) collective-permute-start(bf16[8,2,2048]{2,1,0:T(2,128)(2,1)S(1)} %get-tuple-element.64), channel_id=1, source_target_pairs={{0,1},{1,2},{2,3},{4,5},{5,6},{6,7},{8,9},{9,10},{10,11},{12,13},{... | collective-permute-start | bytes 196616 | tf_op jit(solution)/shard_map/ppermute | solution.py:633
  13.4 1.1 %copy-start.4 = (bf16[8,2,2048]{2,1,0:T(2,128)(2,1)}, bf16[8,2,2048]{2,1,0:T(2,128)(2,1)S(1)}, u32[]{:S(2)}) copy-start(bf16[8,2,2048]{2,1,0:T(2,128)(2,1)S(1)} %collective-permute-done.1.refs_3_) | copy-start | bytes 196612
  14.5 0.6 copy-start.5
  20.3 12.3 %collective-permute-start.6 = (bf16[1120,128]{1,0:T(8,128)(2,1)}, bf16[1120,128]{1,0:T(8,128)(2,1)S(1)}, u32[]{:S(2)}, u32[]{:S(2)}) collective-permute-start(bf16[1120,128]{1,0:T(8,128)(2,1)} %get-tuple-element.49), channel_id=1, source_target_pairs={{0,20},{4,16},{8,28},{12,24},{16,4},{20,0},{24,12},{28,8},{1,21},{... | collective-permute-start | bytes 860168 | tf_op jit(solution)/shard_map/ppermute | solution.py:628
  21.2 20.8 %collective-permute-start.3 = (bf16[1120,128]{1,0:T(8,128)(2,1)}, bf16[1120,128]{1,0:T(8,128)(2,1)S(1)}, u32[]{:S(2)}, u32[]{:S(2)}) collective-permute-start(bf16[1120,128]{1,0:T(8,128)(2,1)} %get-tuple-element.41), channel_id=1, source_target_pairs={{0,4},{4,0},{8,12},{12,8},{16,20},{20,16},{24,28},{28,24},{1,5},{5... | collective-permute-start | bytes 860168 | tf_op jit(solution)/shard_map/ppermute | solution.py:628
  22.4 19.7 %collective-permute-start.9 = (bf16[1120,128]{1,0:T(8,128)(2,1)}, bf16[1120,128]{1,0:T(8,128)(2,1)S(1)}, u32[]{:S(2)}, u32[]{:S(2)}) collective-permute-start(bf16[1120,128]{1,0:T(8,128)(2,1)} %get-tuple-element.55), channel_id=1, source_target_pairs={{0,8},{4,12},{8,0},{12,4},{16,24},{20,28},{24,16},{28,20},{1,9},{5... | collective-permute-start | bytes 860168 | tf_op jit(solution)/shard_map/ppermute | solution.py:628
  22.4 19.6 %collective-permute-start.8 = (bf16[80,128]{1,0:T(8,128)(2,1)}, bf16[80,128]{1,0:T(8,128)(2,1)S(1)}, u32[]{:S(2)}, u32[]{:S(2)}) collective-permute-start(bf16[80,128]{1,0:T(8,128)(2,1)} %get-tuple-element.52), channel_id=1, source_target_pairs={{0,16},{4,20},{8,24},{12,28},{16,0},{20,4},{24,8},{28,12},{1,17},{... | collective-permute-start | bytes 61448 | tf_op jit(solution)/shard_map/ppermute | solution.py:637
  24.0 27.6 %collective-permute-start.5 = (bf16[1120,128]{1,0:T(8,128)(2,1)}, bf16[1120,128]{1,0:T(8,128)(2,1)S(1)}, u32[]{:S(2)}, u32[]{:S(2)}) collective-permute-start(bf16[1120,128]{1,0:T(8,128)(2,1)} %get-tuple-element.47), channel_id=1, source_target_pairs={{0,12},{4,8},{8,4},{12,0},{16,28},{20,24},{24,20},{28,16},{1,13},{... | collective-permute-start | bytes 860168 | tf_op jit(solution)/shard_map/ppermute | solution.py:628
  32.6 20.9 %collective-permute-start.7 = (bf16[1120,128]{1,0:T(8,128)(2,1)}, bf16[1120,128]{1,0:T(8,128)(2,1)S(1)}, u32[]{:S(2)}, u32[]{:S(2)}) collective-permute-start(bf16[1120,128]{1,0:T(8,128)(2,1)} %get-tuple-element.50), channel_id=1, source_target_pairs={{0,24},{4,28},{8,16},{12,20},{16,8},{20,12},{24,0},{28,4},{1,25},{... | collective-permute-start | bytes 860168 | tf_op jit(solution)/shard_map/ppermute | solution.py:628
  34.6 1.0 %copy-start = (bf16[3,544,128]{2,1,0:T(8,128)(2,1)S(1)}, bf16[3,544,128]{2,1,0:T(8,128)(2,1)}, u32[]{:S(2)}) copy-start(bf16[3,544,128]{2,1,0:T(8,128)(2,1)} %get-tuple-element.34.refs_0_) | copy-start | bytes 1253380
  35.6 1.0 %copy-start.2 = (bf16[1120,128]{1,0:T(8,128)(2,1)S(1)}, bf16[1120,128]{1,0:T(8,128)(2,1)}, u32[]{:S(2)}) copy-start(bf16[1120,128]{1,0:T(8,128)(2,1)} %get-tuple-element.56.refs_1_) | copy-start | bytes 860164
  36.6 5.4 %copy-start.3 = (bf16[1120,128]{1,0:T(8,128)(2,1)S(1)}, bf16[1120,128]{1,0:T(8,128)(2,1)}, u32[]{:S(2)}) copy-start(bf16[1120,128]{1,0:T(8,128)(2,1)} %get-tuple-element.42) | copy-start | bytes 860164
  36.6 5.5 %copy-start.1 = (bf16[3,544,128]{2,1,0:T(8,128)(2,1)S(1)}, bf16[3,544,128]{2,1,0:T(8,128)(2,1)}, u32[]{:S(2)}) copy-start(bf16[3,544,128]{2,1,0:T(8,128)(2,1)} %get-tuple-element.34.refs_0_) | copy-start | bytes 1253380
  42.0 19.8 %collective-permute-start.4 = (bf16[1120,128]{1,0:T(8,128)(2,1)S(1)}, bf16[1120,128]{1,0:T(8,128)(2,1)S(1)}, u32[]{:S(2)}, u32[]{:S(2)}) collective-permute-start(bf16[1120,128]{1,0:T(8,128)(2,1)S(1)} %copy-done.3), channel_id=1, source_target_pairs={{0,28},{4,24},{8,20},{12,16},{16,12},{20,8},{24,4},{28,0},{1,29},{... | collective-permute-start | bytes 860168 | tf_op jit(solution)/shard_map/ppermute | solution.py:628

commit v5 on v4

--- a/solution.py
+++ b/solution.py
@@ -98,7 +98,7 @@
             return tuple(result)
 
         first, last = part * FOLD, min((part + 1) * FOLD, outs_pairs)
-        unroll = 4 if (last - first) % 4 == 0 else 1
+        unroll = 8 if (last - first) % 8 == 0 else 1
         edges = lax.fori_loop(first, last, pair, (zero,) * len(outs), unroll=unroll)
         for (own, _, _), out, edge in zip(places, outs, edges):
             start = len(own) * span + part * PAIR

time: 67.5 us -> 67.3 us (level)
  no operation moved by 1% of the time
where the time goes in v5:
time: 67.3 us; the launch traced here: 66.7 us
  Pallas kernels  30 us (45%)
  waiting for transfers between devices  17.2 us (26%)
  starting transfers between devices  15.1 us (22%)
  local copies, waits for them, and re-layouts  3.72 us (6%)
    pallas_call x4, Pallas kernels, lag_sums(): pl.pallas_call(lambda *refs: lag_kernel(tiles, rows, frames, counts, prio...  22.2 us
    ppermute x7, waiting for transfers between devices, send(): lax.ppermute(payload, 'frame', [(i, i ^ k) for i in range(peers)])  15.9 us
    ppermute x7, starting transfers between devices, send(): lax.ppermute(payload, 'frame', [(i, i ^ k) for i in range(peers)])  7.79 us
    pallas_call x1, Pallas kernels, pack_rest(): pl.pallas_call(lambda *refs: pack_kernel(tiles, skip, *refs), out_shape=[...  4.85 us
    ppermute x1, starting transfers between devices, body(): above = lax.ppermute(last, 'strip', up)  3.05 us
    pallas_call x1, Pallas kernels, pack_one(): pl.pallas_call(lambda *refs: pack_one_kernel(tiles, *refs), out_shape=jax...  2.93 us
    ppermute x1, starting transfers between devices, body(): below = lax.ppermute(initial, 'strip', down)  2.86 us
    unnamed x12, local copies, waits for them, and re-layouts  2.58 us
  transfers between devices with their start and end apart: 10, of which 6 were waited for; matrix products, arithmetic and copies ran while one was open for 2% of the time, Pallas kernels for 33%

profile of v5, /device:TPU:11, one launch (start us, length us, event | category | flops | bytes accessed | tf_op | source)
XLA Modules:
  0.0 66.7 jit_solution(11461822623776468636)
XLA Ops:
  0.0 0.7 pad_add_fusion.refs_0_
  0.7 2.9 %pack_one.1 = bf16[1040,128]{1,0:T(8,128)(2,1)} custom-call(s32[2]{0:T(128)} %pad_add_fusion.refs_0_, bf16[8,64,2048]{2,1,0:T(8,128)(2,1)} %refs_3_.1, bf16[8,64,2048]{2,1,0:T(8,128)(2,1)} %refs_3_.1, bf16[8,64,2048]{2,1,0:T(8,128)(2,1)} %refs_3_.1), custom_call_target="tpu_custom_call" | custom-call | flops 900000000 | bytes 3000000 | tf_op jit(solution)/shard_map/pack_one/pallas_call | solution.py:138
  3.6 2.3 %collective-permute-start.2 = (bf16[1040,128]{1,0:T(8,128)(2,1)}, bf16[1040,128]{1,0:T(8,128)(2,1)S(1)}, u32[]{:S(2)}, u32[]{:S(2)}) collective-permute-start(bf16[1040,128]{1,0:T(8,128)(2,1)} %pack_one.1), channel_id=1, source_target_pairs={{0,16},{4,20},{8,24},{12,28},{16,0},{20,4},{24,8},{28,12},{1,17},{... | collective-permute-start | bytes 798728 | tf_op jit(solution)/shard_map/ppermute | solution.py:628
  5.9 1.1 %fusion = (bf16[8,2,2048]{2,1,0:T(2,128)(2,1)S(1)}, bf16[8,2,2048]{2,1,0:T(2,128)(2,1)S(1)}) fusion(bf16[8,64,2048]{2,1,0:T(8,128)(2,1)} %refs_3_.1), kind=kLoop, calls=%fused_computation.1 | loop fusion | bytes 262144 | tf_op jit(solution)/shard_map/slice | solution.py:632
  7.0 2.9 %collective-permute-start.1 = (bf16[8,2,2048]{2,1,0:T(2,128)(2,1)S(1)}, bf16[8,2,2048]{2,1,0:T(2,128)(2,1)S(1)}, u32[]{:S(2)}, u32[]{:S(2)}) collective-permute-start(bf16[8,2,2048]{2,1,0:T(2,128)(2,1)S(1)} %get-tuple-element.63), channel_id=1, source_target_pairs={{1,0},{2,1},{3,2},{5,4},{6,5},{7,6},{9,8},{10,9},{11,10},{13,12},{... | collective-permute-start | bytes 196616 | tf_op jit(solution)/shard_map/ppermute | solution.py:634
  9.9 3.0 %collective-permute-start = (bf16[8,2,2048]{2,1,0:T(2,128)(2,1)S(1)}, bf16[8,2,2048]{2,1,0:T(2,128)(2,1)S(1)}, u32[]{:S(2)}, u32[]{:S(2)}) collective-permute-start(bf16[8,2,2048]{2,1,0:T(2,128)(2,1)S(1)} %get-tuple-element.64), channel_id=1, source_target_pairs={{0,1},{1,2},{2,3},{4,5},{5,6},{6,7},{8,9},{9,10},{10,11},{12,13},{... | collective-permute-start | bytes 196616 | tf_op jit(solution)/shard_map/ppermute | solution.py:633
  12.9 0.2 collective-permute-done.1.refs_3_
  13.2 0.0 copy-start.4
  13.2 1.1 %collective-permute-done.refs_2_ = bf16[8,2,2048]{2,1,0:T(2,128)(2,1)S(1)} collective-permute-done((bf16[8,2,2048]{2,1,0:T(2,128)(2,1)S(1)}, bf16[8,2,2048]{2,1,0:T(2,128)(2,1)S(1)}, u32[]{:S(2)}, u32[]{:S(2)}) %collective-permute-start) | collective-permute-done | bytes 65568 | tf_op jit(solution)/shard_map/ppermute | solution.py:633
  14.3 0.0 copy-start.5
  14.3 0.0 copy-done.4
  14.3 0.6 copy-done.5
  14.9 4.8 %pack_rest.1 = (bf16[1120,128]{1,0:T(8,128)(2,1)}, bf16[1120,128]{1,0:T(8,128)(2,1)}, bf16[1120,128]{1,0:T(8,128)(2,1)}, bf16[1120,128]{1,0:T(8,128)(2,1)}, bf16...) custom-call(s32[1]{0:T(128)} %bitcast.refs_0_, ...), custom_call_target="tpu_custom_call" | custom-call | flops 1500000000 | bytes 5000000 | tf_op jit(solution)/shard_map/pack_rest/pallas_call | solution.py:233
  19.7 0.0 collective-permute-done.2.refs_1_
  19.7 1.2 %collective-permute-start.6 = (bf16[1120,128]{1,0:T(8,128)(2,1)}, bf16[1120,128]{1,0:T(8,128)(2,1)S(1)}, u32[]{:S(2)}, u32[]{:S(2)}) collective-permute-start(bf16[1120,128]{1,0:T(8,128)(2,1)} %get-tuple-element.49), channel_id=1, source_target_pairs={{0,20},{4,16},{8,28},{12,24},{16,4},{20,0},{24,12},{28,8},{1,21},{... | collective-permute-start | bytes 860168 | tf_op jit(solution)/shard_map/ppermute | solution.py:628
  20.9 1.2 %collective-permute-start.3 = (bf16[1120,128]{1,0:T(8,128)(2,1)}, bf16[1120,128]{1,0:T(8,128)(2,1)S(1)}, u32[]{:S(2)}, u32[]{:S(2)}) collective-permute-start(bf16[1120,128]{1,0:T(8,128)(2,1)} %get-tuple-element.41), channel_id=1, source_target_pairs={{0,4},{4,0},{8,12},{12,8},{16,20},{20,16},{24,28},{28,24},{1,5},{5... | collective-permute-start | bytes 860168 | tf_op jit(solution)/shard_map/ppermute | solution.py:628
  22.1 0.0 collective-permute-start.9
  22.1 1.4 %collective-permute-start.8 = (bf16[80,128]{1,0:T(8,128)(2,1)}, bf16[80,128]{1,0:T(8,128)(2,1)S(1)}, u32[]{:S(2)}, u32[]{:S(2)}) collective-permute-start(bf16[80,128]{1,0:T(8,128)(2,1)} %get-tuple-element.52), channel_id=1, source_target_pairs={{0,16},{4,20},{8,24},{12,28},{16,0},{20,4},{24,8},{28,12},{1,17},{... | collective-permute-start | bytes 61448 | tf_op jit(solution)/shard_map/ppermute | solution.py:637
  23.4 1.3 %collective-permute-start.5 = (bf16[1120,128]{1,0:T(8,128)(2,1)}, bf16[1120,128]{1,0:T(8,128)(2,1)S(1)}, u32[]{:S(2)}, u32[]{:S(2)}) collective-permute-start(bf16[1120,128]{1,0:T(8,128)(2,1)} %get-tuple-element.47), channel_id=1, source_target_pairs={{0,12},{4,8},{8,4},{12,0},{16,28},{20,24},{24,20},{28,16},{1,13},{... | collective-permute-start | bytes 860168 | tf_op jit(solution)/shard_map/ppermute | solution.py:628
  24.7 7.6 %collective-permute-done.6.refs_3_ = bf16[1120,128]{1,0:T(8,128)(2,1)S(1)} collective-permute-done((bf16[1120,128]{1,0:T(8,128)(2,1)}, bf16[1120,128]{1,0:T(8,128)(2,1)S(1)}, u32[]{:S(2)}, u32[]{:S(2)}) %collective-permute-start.6) | collective-permute-done | bytes 286752 | tf_op jit(solution)/shard_map/ppermute | solution.py:628
  32.4 1.9 %collective-permute-start.7 = (bf16[1120,128]{1,0:T(8,128)(2,1)}, bf16[1120,128]{1,0:T(8,128)(2,1)S(1)}, u32[]{:S(2)}, u32[]{:S(2)}) collective-permute-start(bf16[1120,128]{1,0:T(8,128)(2,1)} %get-tuple-element.50), channel_id=1, source_target_pairs={{0,24},{4,28},{8,16},{12,20},{16,8},{20,12},{24,0},{28,4},{1,25},{... | collective-permute-start | bytes 860168 | tf_op jit(solution)/shard_map/ppermute | solution.py:628
  34.2 0.0 copy-start
  34.2 1.0 %copy-done = bf16[3,544,128]{2,1,0:T(8,128)(2,1)S(1)} copy-done((bf16[3,544,128]{2,1,0:T(8,128)(2,1)S(1)}, bf16[3,544,128]{2,1,0:T(8,128)(2,1)}, u32[]{:S(2)}) %copy-start) | copy-done | bytes 417816
  35.2 0.0 copy-start.2
  35.2 1.0 %copy-done.2 = bf16[1120,128]{1,0:T(8,128)(2,1)S(1)} copy-done((bf16[1120,128]{1,0:T(8,128)(2,1)S(1)}, bf16[1120,128]{1,0:T(8,128)(2,1)}, u32[]{:S(2)}) %copy-start.2) | copy-done | bytes 286744
  36.2 0.0 copy-start.3
  36.2 0.0 copy-start.1
  36.2 2.9 %lag_sums.3 = (f32[13,3,72,128]{3,2,1,0:T(8,128)S(1)}, f32[3,80,128]{2,1,0:T(8,128)S(1)}) custom-call(bf16[3,544,128]{2,1,0:T(8,128)(2,1)S(1)} %copy-done, bf16[1120,128]{1,0:T(8,128)(2,1)S(1)} %copy-done.2), custom_call_target="tpu_custom_call" | custom-call | flops 1200000000 | bytes 4000000 | tf_op jit(solution)/shard_map/lag_sums/pallas_call | solution.py:595
  39.1 3.0 %collective-permute-done.3.refs_4_ = bf16[1120,128]{1,0:T(8,128)(2,1)S(1)} collective-permute-done((bf16[1120,128]{1,0:T(8,128)(2,1)}, bf16[1120,128]{1,0:T(8,128)(2,1)S(1)}, u32[]{:S(2)}, u32[]{:S(2)}) %collective-permute-start.3) | collective-permute-done | bytes 286752 | tf_op jit(solution)/shard_map/ppermute | solution.py:628
  42.1 0.0 copy-done.3
  42.1 0.0 collective-permute-start.4
  42.1 0.0 collective-permute-done.8.refs_2_
  42.1 0.0 collective-permute-done.9.refs_5_
  42.1 0.0 copy-done.1
  42.1 9.6 %lag_sums.4 = (f32[13,3,72,128]{3,2,1,0:T(8,128)S(1)}, f32[3,80,128]{2,1,0:T(8,128)S(1)}) custom-call(bf16[3,544,128]{2,1,0:T(8,128)(2,1)S(1)} %copy-done.1, bf16[1040,128]{1,0:T(8,128)(2,1)S(1)} %collective-permute-done.2.refs_1_, bf16[80,128]{1,0:T(8,128)(2,1)S(1)} %collective-permute-done.8.refs_2_, bf16[1120,128]{1,0:T(8,128)(2,1)S(1)} %collective-permute-done.6.refs_3_, ...), custom_call_target="tpu_custom_call" | custom-call | flops 3000000000 | bytes 10000000 | tf_op jit(solution)/shard_map/lag_sums/pallas_call | solution.py:595
  51.7 0.0 collective-permute-done.5.refs_1_
  51.7 1.2 %collective-permute-done.7.refs_2_ = bf16[1120,128]{1,0:T(8,128)(2,1)S(1)} collective-permute-done((bf16[1120,128]{1,0:T(8,128)(2,1)}, bf16[1120,128]{1,0:T(8,128)(2,1)S(1)}, u32[]{:S(2)}, u32[]{:S(2)}) %collective-permute-start.7) | collective-permute-done | bytes 286752 | tf_op jit(solution)/shard_map/ppermute | solution.py:628
  52.9 4.4 %lag_sums.5 = (f32[13,3,72,128]{3,2,1,0:T(8,128)S(1)}, f32[3,80,128]{2,1,0:T(8,128)S(1)}) custom-call(bf16[3,544,128]{2,1,0:T(8,128)(2,1)S(1)} %copy-done.1, bf16[1120,128]{1,0:T(8,128)(2,1)S(1)} %collective-permute-done.5.refs_1_, bf16[1120,128]{1,0:T(8,128)(2,1)S(1)} %collective-permute-done.7.refs_2_, f32[13,3,72,128]{3,2,1,0:T(8,128)S(1)} %get-tuple-element.59.refs_3_, ...), custom_call_target="tpu_custom_call" | custom-call | flops 1800000000 | bytes 6000000 | tf_op jit(solution)/shard_map/lag_sums/pallas_call | solution.py:595
  57.3 4.0 %collective-permute-done.4.refs_1_ = bf16[1120,128]{1,0:T(8,128)(2,1)S(1)} collective-permute-done((bf16[1120,128]{1,0:T(8,128)(2,1)S(1)}, bf16[1120,128]{1,0:T(8,128)(2,1)S(1)}, u32[]{:S(2)}, u32[]{:S(2)}) %collective-permute-start.4) | collective-permute-done | bytes 286752 | tf_op jit(solution)/shard_map/ppermute | solution.py:628
  61.4 5.4 %lag_maps.1 = f32[25,64,256]{2,1,0:T(8,128)} custom-call(bf16[3,544,128]{2,1,0:T(8,128)(2,1)S(1)} %copy-done.1, bf16[1120,128]{1,0:T(8,128)(2,1)S(1)} %collective-permute-done.4.refs_1_, f32[13,3,72,128]{3,2,1,0:T(8,128)S(1)} %get-tuple-element.61.refs_2_, f32[3,80,128]{2,1,0:T(8,128)S(1)} %get-tuple-element.62.refs_3_), custom_call_target="tpu_custom_call" | custom-call | flops 1200000000 | bytes 4000000 | tf_op jit(solution)/shard_map/lag_maps/pallas_call | solution.py:595
Async XLA Ops:
  3.6 16.1 %collective-permute-start.2 = (bf16[1040,128]{1,0:T(8,128)(2,1)}, bf16[1040,128]{1,0:T(8,128)(2,1)S(1)}, u32[]{:S(2)}, u32[]{:S(2)}) collective-permute-start(bf16[1040,128]{1,0:T(8,128)(2,1)} %pack_one.1), channel_id=1, source_target_pairs={{0,16},{4,20},{8,24},{12,28},{16,0},{20,4},{24,8},{28,12},{1,17},{... | collective-permute-start | bytes 798728 | tf_op jit(solution)/shard_map/ppermute | solution.py:628
  7.0 6.1 %collective-permute-start.1 = (bf16[8,2,2048]{2,1,0:T(2,128)(2,1)S(1)}, bf16[8,2,2048]{2,1,0:T(2,128)(2,1)S(1)}, u32[]{:S(2)}, u32[]{:S(2)}) collective-permute-start(bf16[8,2,2048]{2,1,0:T(2,128)(2,1)S(1)} %get-tuple-element.63), channel_id=1, source_target_pairs={{1,0},{2,1},{3,2},{5,4},{6,5},{7,6},{9,8},{10,9},{11,10},{13,12},{... | collective-permute-start | bytes 196616 | tf_op jit(solution)/shard_map/ppermute | solution.py:634
  9.9 4.4 %collective-permute-start = (bf16[8,2,2048]{2,1,0:T(2,128)(2,1)S(1)}, bf16[8,2,2048]{2,1,0:T(2,128)(2,1)S(1)}, u32[]{:S(2)}, u32[]{:S(2)}) collective-permute-start(bf16[8,2,2048]{2,1,0:T(2,128)(2,1)S(1)} %get-tuple-element.64), channel_id=1, source_target_pairs={{0,1},{1,2},{2,3},{4,5},{5,6},{6,7},{8,9},{9,10},{10,11},{12,13},{... | collective-permute-start | bytes 196616 | tf_op jit(solution)/shard_map/ppermute | solution.py:633
  13.2 1.1 %copy-start.4 = (bf16[8,2,2048]{2,1,0:T(2,128)(2,1)}, bf16[8,2,2048]{2,1,0:T(2,128)(2,1)S(1)}, u32[]{:S(2)}) copy-start(bf16[8,2,2048]{2,1,0:T(2,128)(2,1)S(1)} %collective-permute-done.1.refs_3_) | copy-start | bytes 196612
  14.3 0.6 copy-start.5
  19.7 12.6 %collective-permute-start.6 = (bf16[1120,128]{1,0:T(8,128)(2,1)}, bf16[1120,128]{1,0:T(8,128)(2,1)S(1)}, u32[]{:S(2)}, u32[]{:S(2)}) collective-permute-start(bf16[1120,128]{1,0:T(8,128)(2,1)} %get-tuple-element.49), channel_id=1, source_target_pairs={{0,20},{4,16},{8,28},{12,24},{16,4},{20,0},{24,12},{28,8},{1,21},{... | collective-permute-start | bytes 860168 | tf_op jit(solution)/shard_map/ppermute | solution.py:628
  20.9 21.2 %collective-permute-start.3 = (bf16[1120,128]{1,0:T(8,128)(2,1)}, bf16[1120,128]{1,0:T(8,128)(2,1)S(1)}, u32[]{:S(2)}, u32[]{:S(2)}) collective-permute-start(bf16[1120,128]{1,0:T(8,128)(2,1)} %get-tuple-element.41), channel_id=1, source_target_pairs={{0,4},{4,0},{8,12},{12,8},{16,20},{20,16},{24,28},{28,24},{1,5},{5... | collective-permute-start | bytes 860168 | tf_op jit(solution)/shard_map/ppermute | solution.py:628
  22.1 20.0 %collective-permute-start.9 = (bf16[1120,128]{1,0:T(8,128)(2,1)}, bf16[1120,128]{1,0:T(8,128)(2,1)S(1)}, u32[]{:S(2)}, u32[]{:S(2)}) collective-permute-start(bf16[1120,128]{1,0:T(8,128)(2,1)} %get-tuple-element.55), channel_id=1, source_target_pairs={{0,8},{4,12},{8,0},{12,4},{16,24},{20,28},{24,16},{28,20},{1,9},{5... | collective-permute-start | bytes 860168 | tf_op jit(solution)/shard_map/ppermute | solution.py:628
  22.1 20.0 %collective-permute-start.8 = (bf16[80,128]{1,0:T(8,128)(2,1)}, bf16[80,128]{1,0:T(8,128)(2,1)S(1)}, u32[]{:S(2)}, u32[]{:S(2)}) collective-permute-start(bf16[80,128]{1,0:T(8,128)(2,1)} %get-tuple-element.52), channel_id=1, source_target_pairs={{0,16},{4,20},{8,24},{12,28},{16,0},{20,4},{24,8},{28,12},{1,17},{... | collective-permute-start | bytes 61448 | tf_op jit(solution)/shard_map/ppermute | solution.py:637
  23.4 28.2 %collective-permute-start.5 = (bf16[1120,128]{1,0:T(8,128)(2,1)}, bf16[1120,128]{1,0:T(8,128)(2,1)S(1)}, u32[]{:S(2)}, u32[]{:S(2)}) collective-permute-start(bf16[1120,128]{1,0:T(8,128)(2,1)} %get-tuple-element.47), channel_id=1, source_target_pairs={{0,12},{4,8},{8,4},{12,0},{16,28},{20,24},{24,20},{28,16},{1,13},{... | collective-permute-start | bytes 860168 | tf_op jit(solution)/shard_map/ppermute | solution.py:628
  32.4 20.6 %collective-permute-start.7 = (bf16[1120,128]{1,0:T(8,128)(2,1)}, bf16[1120,128]{1,0:T(8,128)(2,1)S(1)}, u32[]{:S(2)}, u32[]{:S(2)}) collective-permute-start(bf16[1120,128]{1,0:T(8,128)(2,1)} %get-tuple-element.50), channel_id=1, source_target_pairs={{0,24},{4,28},{8,16},{12,20},{16,8},{20,12},{24,0},{28,4},{1,25},{... | collective-permute-start | bytes 860168 | tf_op jit(solution)/shard_map/ppermute | solution.py:628
  34.2 1.0 %copy-start = (bf16[3,544,128]{2,1,0:T(8,128)(2,1)S(1)}, bf16[3,544,128]{2,1,0:T(8,128)(2,1)}, u32[]{:S(2)}) copy-start(bf16[3,544,128]{2,1,0:T(8,128)(2,1)} %get-tuple-element.34.refs_0_) | copy-start | bytes 1253380
  35.2 1.0 %copy-start.2 = (bf16[1120,128]{1,0:T(8,128)(2,1)S(1)}, bf16[1120,128]{1,0:T(8,128)(2,1)}, u32[]{:S(2)}) copy-start(bf16[1120,128]{1,0:T(8,128)(2,1)} %get-tuple-element.56.refs_1_) | copy-start | bytes 860164
  36.2 5.9 %copy-start.3 = (bf16[1120,128]{1,0:T(8,128)(2,1)S(1)}, bf16[1120,128]{1,0:T(8,128)(2,1)}, u32[]{:S(2)}) copy-start(bf16[1120,128]{1,0:T(8,128)(2,1)} %get-tuple-element.42) | copy-start | bytes 860164
  36.2 5.9 %copy-start.1 = (bf16[3,544,128]{2,1,0:T(8,128)(2,1)S(1)}, bf16[3,544,128]{2,1,0:T(8,128)(2,1)}, u32[]{:S(2)}) copy-start(bf16[3,544,128]{2,1,0:T(8,128)(2,1)} %get-tuple-element.34.refs_0_) | copy-start | bytes 1253380
  42.1 19.3 %collective-permute-start.4 = (bf16[1120,128]{1,0:T(8,128)(2,1)S(1)}, bf16[1120,128]{1,0:T(8,128)(2,1)S(1)}, u32[]{:S(2)}, u32[]{:S(2)}) collective-permute-start(bf16[1120,128]{1,0:T(8,128)(2,1)S(1)} %copy-done.3), channel_id=1, source_target_pairs={{0,28},{4,24},{8,20},{12,16},{16,12},{20,8},{24,4},{28,0},{1,29},{... | collective-permute-start | bytes 860168 | tf_op jit(solution)/shard_map/ppermute | solution.py:628
